TPU v7x, 128 devices: a whole 4x4x4 slice. The times are simulated.
128 devices in a mesh: dp: 8 (over x_lo, y), seq: 16 (over z, x_hi, core).
Axes of the slice: x: 4 (x_hi: 2, x_lo: 2; x = x_hi * 2 + x_lo), y: 4, z: 4, core: 2. Of those that a mesh axis runs over, the one named last changes fastest.
Arguments:
- tokens: bfloat16 [8, 4096, 768], P('dp', 'seq'), may hold values from -6 to 6
- segment_ids: int32 [8, 4096], P('dp', 'seq'), may hold values from 0 to 16, as said below
- norm_one: bfloat16 [768], P(('dp', 'seq')), may hold values from 0.5 to 1.5
- qkv_weight: bfloat16 [768, 2304], P(('dp', 'seq')), may hold values from -0.21875 to 0.21875
- out_weight: bfloat16 [768, 768], P(('dp', 'seq')), may hold values from -2.5 to 2.5
- norm_two: bfloat16 [768], P(('dp', 'seq')), may hold values from 0.5 to 1.5
- in_weight: bfloat16 [768, 2304], P(('dp', 'seq')), may hold values from -0.21875 to 0.21875
- down_weight: bfloat16 [1152, 768], P(('dp', 'seq')), may hold values from -0.375 to 0.375
- cotangent: bfloat16 [8, 4096, 768], P('dp', 'seq'), may hold values from -6 to 6
Outputs:
- mixed: bfloat16 [8, 4096, 768], P('dp', 'seq')
- input_grad: bfloat16 [8, 4096, 768], P('dp', 'seq')
- norm_one_grad: float32 [768], P(('dp', 'seq'))
- qkv_weight_grad: float32 [768, 2304], P(('dp', 'seq'))
- out_weight_grad: float32 [768, 768], P(('dp', 'seq'))
- norm_two_grad: float32 [768], P(('dp', 'seq'))
- in_weight_grad: float32 [768, 2304], P(('dp', 'seq'))
- down_weight_grad: float32 [1152, 768], P(('dp', 'seq'))
Inputs may be any that keep to these rules, and one draw needn't show every extreme that they name: `segment_ids`: ids are 0 at the first token of each sequence, never fall, and rise by one at the first token of each new document; every document after the first, except the last of a sequence, has 256 tokens or more.
All inputs are finite; a program needn't handle non-finite values.
Results may differ from a plain program's by a relative error of at most 0.022.
Values may be sent and summed in bfloat16 or wider, within the bound.
No kernel may reach another device: no remote copies, remote signals or barrier semaphores. Data moves between devices by JAX's collectives and lax.ppermute only.
A program may use at most 128 MiB of HBM per device.

v0:
```python
import math

import jax
import jax.numpy as jnp
from jax import lax
from jax.experimental import pallas as pl
from jax.experimental.pallas import tpu as pltpu
from jax.sharding import Mesh, PartitionSpec as P

HEAD = 64
HALF = 64
AXES = ("x_lo", "y", "z", "x_hi", "core")
DP = ("x_lo", "y")
SEQ = ("z", "x_hi", "core")
X = ("x_lo", "x_hi")
F32 = jnp.float32
BF16 = jnp.bfloat16


def swap_cores(value):
    return lax.ppermute(value, "core", [(0, 1), (1, 0)])


def line_send(value, axis, step):
    if axis == "x":
        return lax.ppermute(value, X, [(i, i ^ step) for i in range(4)])
    return lax.ppermute(value, axis, [(i, (i + step) % 4) for i in range(4)])


def line_gather(block, axis):
    return [block] + [line_send(block, axis, step) for step in (1, 2, 3)]


def line_sum(values, axis):
    rows = values.shape[0] // 4
    total = values[:rows]
    for step in (1, 2, 3):
        part = values[rows * step : rows * step + rows].astype(BF16)
        total = total + line_send(part, axis, step if axis == "x" else 4 - step).astype(F32)
    return total


def owner_rows(first):
    index = jnp.arange(768, dtype=jnp.int32)
    core = (index // 384) ^ lax.axis_index("core")
    step, turn = (index // 96) % 4, (index // 24) % 4
    if first == "y":
        step, turn = turn, step
    line = (lax.axis_index("x_lo") * 2 + lax.axis_index("x_hi")) ^ step
    y = (lax.axis_index("y") - turn) % 4
    z = (lax.axis_index("z") - (index // 6) % 4) % 4
    device = (((line // 2) * 4 + y) * 4 + z) * 4 + (line % 2) * 2 + core
    return device * 6 + index % 6


def chooser(natural, count=768):
    return (jnp.arange(count, dtype=jnp.int32)[:, None] == natural[None, :]).astype(BF16)


def down_choosers(natural):
    device, row = natural // 6, natural % 6
    late = device * 9 + 6 + row // 2
    return (
        chooser(device * 9 + row, 1152),
        chooser(jnp.where(row % 2 == 0, late, -1), 1152),
        chooser(jnp.where(row % 2 == 1, late, -1), 1152),
    )


def dot(a, b):
    return jnp.dot(a, b, preferred_element_type=F32)


def dot_nt(a, b):
    return lax.dot_general(a, b, (((1,), (1,)), ((), ())), preferred_element_type=F32)


def dot_tn(a, b):
    return lax.dot_general(a, b, (((0,), (0,)), ((), ())), preferred_element_type=F32)


def unit_rows(dtype=BF16):
    row = lax.broadcasted_iota(jnp.int32, (8, 128), 0)
    lane = lax.broadcasted_iota(jnp.int32, (8, 128), 1)
    return (row == lane).astype(F32).astype(dtype)


def normed(values):
    centred = values - jnp.mean(values, -1, keepdims=True)
    scale = lax.rsqrt(jnp.mean(centred * centred, -1, keepdims=True) + 1e-05)
    return centred * scale, scale


def norm_back(grad, gain, unit, scale):
    e = grad * gain
    return scale * (
        e - jnp.mean(e, -1, keepdims=True) - unit * jnp.mean(e * unit, -1, keepdims=True)
    )


def wide(table, count):
    return jnp.concatenate([table] * count, 1)


def half_turn(values):
    lane = lax.broadcasted_iota(jnp.int32, values.shape, 1) % HEAD
    size = values.shape[1]
    after = pltpu.roll(values, size - HEAD // 2, 1)
    before = pltpu.roll(values, HEAD // 2, 1)
    return jnp.where(lane < HEAD // 2, -after, before)


def rotate(values, cosine, sine):
    return values * cosine + half_turn(values) * sine


def rotate_back(values, cosine, sine):
    return values * cosine - half_turn(values * sine)


def project_kernel(*refs):
    pieces = refs[:8]
    tokens, choose, cosine, sine, marks = refs[8:13]
    queries, key_values, ordered, gains, weight, sems = refs[13:]
    copies = load_pieces(pieces, weight, sems, 0)
    unit, _ = normed(tokens[...].astype(F32))
    wait_all(copies)
    gain_order = dot_nt(unit_rows(), weight[:, 2304:]).astype(BF16)
    gain = dot_nt(gain_order, choose[...])
    gains[...] = gain
    h_one = (unit * gain[0:1]).astype(BF16)
    h_ord = dot(h_one, choose[...]).astype(BF16)
    ordered[...] = h_ord
    cos_w, sin_w = wide(cosine[...], 6), wide(sine[...], 6)
    part = dot(h_ord, weight[:, :768])
    queries[...] = rotate(part, cos_w, sin_w).astype(BF16)
    part = dot(h_ord, weight[:, 768:1536])
    key_values[:, :768] = rotate(part, cos_w, sin_w).astype(BF16)
    part = dot(h_ord, weight[:, 1536:2304])
    key_values[:, 768:1536] = part.astype(BF16)
    key_values[:, 1536:] = marks[...]


def load_pieces(pieces, target, sems, first):
    cols = pl.ds(first, target.shape[1])
    copies = []
    for index, piece in enumerate(pieces):
        rows = piece.shape[0]
        copy = pltpu.make_async_copy(
            piece.at[:, cols], target.at[pl.ds(index * rows, rows)], sems.at[index]
        )
        copy.start()
        copies.append(copy)
    return copies


def wait_all(copies):
    for copy in copies:
        copy.wait()


def fill_span(span, prev, key_values, follow):
    span[:64] = prev[...]
    span[64:320] = key_values[...]
    span[320:] = follow[...]


def visible(span, block):
    row = lax.broadcasted_iota(jnp.int32, (128, 256), 0)
    col = lax.broadcasted_iota(jnp.int32, (128, 256), 1)
    gap = col - row
    first = block * 128
    key_marks = dot_nt(unit_rows(), span[first : first + 256, 1536:])[0:1]
    query_marks = span[first + 64 : first + 192, 1536:1537].astype(F32)
    seen = (gap >= 0) & (gap <= 2 * HALF) & (query_marks == key_marks)
    bias = jnp.where(seen, 0.0, -1e30)
    return jnp.concatenate([bias, bias], 0)


def head_stack(values):
    lane = lax.broadcasted_iota(jnp.int32, values.shape, 1)
    zero = jnp.zeros_like(values)
    return jnp.concatenate(
        [jnp.where(lane < HEAD, values, zero), jnp.where(lane >= HEAD, values, zero)], 0
    )


def head_merge(stacked):
    lane = lax.broadcasted_iota(jnp.int32, (128, 128), 1)
    return jnp.where(lane < HEAD, stacked[:128], stacked[128:])


def probabilities(query_stack, keys, bias):
    scores = dot_nt(query_stack, keys) * 0.125 + bias
    expo = jnp.exp(scores - jnp.max(scores, -1, keepdims=True))
    return expo / jnp.sum(expo, -1, keepdims=True)


def attend_kernel(*refs):
    pieces = refs[:8]
    queries, key_values, prev, follow, tokens, choose = refs[8:14]
    ordered, after, span, context, weight, sems = refs[14:]
    copies = load_pieces(pieces, weight, sems, 2304)
    fill_span(span, prev, key_values, follow)
    for block in range(2):
        bias = visible(span, block)
        rows = slice(block * 128, block * 128 + 128)
        cols = slice(block * 128, block * 128 + 256)
        for pair in range(6):
            lanes = slice(pair * 128, pair * 128 + 128)
            value_lanes = slice(768 + pair * 128, 768 + pair * 128 + 128)
            probs = probabilities(head_stack(queries[rows, lanes]), span[cols, lanes], bias)
            mixed = dot(probs.astype(BF16), span[cols, value_lanes])
            context[rows, lanes] = head_merge(mixed).astype(BF16)
    ordered[...] = dot(context[...], choose[...]).astype(BF16)
    wait_all(copies)
    after[...] = tokens[...].astype(F32) + dot(ordered[...], weight[...])


def feed_kernel(*refs):
    pieces = refs[:8]
    after, gains, cotangent, context, choose_in, choose_one, choose_two, choose_three = refs[8:16]
    mixed, grad_own, grad_other, grad_after, gain_grad, weight, d_ref, sems = refs[16:]
    copies = load_pieces(pieces, weight, sems, 0)
    x_two = after[...]
    unit, scale = normed(x_two)
    gain = gains[1:2]
    h_two = (unit * gain).astype(BF16)
    h_ord = dot(h_two, choose_in[...]).astype(BF16)
    wait_all(copies)
    gate = dot(h_ord, weight[:, :1152])
    up = dot(h_ord, weight[:, 1152:2304])
    phi = 0.5 + 0.5 * lax.erf(gate * (2.0**-0.5))
    slope = phi + gate * jnp.exp(-0.5 * gate * gate) * ((2.0 * math.pi) ** -0.5)
    gated = gate * phi
    hidden = (gated * up).astype(BF16)
    hid_one = dot(hidden, choose_one[...]).astype(BF16)
    hid_two = dot(hidden, choose_two[...]).astype(BF16)
    hid_three = dot(hidden, choose_three[...]).astype(BF16)
    main = dot(hid_one, weight[:, 3072:3840])
    mixed[:, :384] = (x_two[:, :384] + main[:, :384] + dot(hid_two, weight[:, 3840:])).astype(BF16)
    mixed[:, 384:] = (x_two[:, 384:] + main[:, 384:] + dot(hid_three, weight[:, 3840:])).astype(
        BF16
    )
    dy = cotangent[...]
    first, second = dy[:, :384], dy[:, 384:]
    halves = ((grad_own, slice(0, 384)), (grad_other, slice(384, 768)))
    for target, part in halves:
        target[:, 3072:3840] = dot_tn(hid_one[:, part], dy).astype(BF16)
        target[:, 3840:] = (
            dot_tn(hid_two[:, part], first) + dot_tn(hid_three[:, part], second)
        ).astype(BF16)
    d_hidden = (
        dot_nt(dot_nt(dy, weight[:, 3072:3840]).astype(BF16), choose_one[...])
        + dot_nt(dot_nt(first, weight[:, 3840:]).astype(BF16), choose_two[...])
        + dot_nt(dot_nt(second, weight[:, 3840:]).astype(BF16), choose_three[...])
    )
    d_ref[:, :1152] = (d_hidden * up * slope).astype(BF16)
    d_ref[:, 1152:] = (d_hidden * gated).astype(BF16)
    for target, part in halves:
        target[:, :2304] = dot_tn(h_ord[:, part], d_ref[...]).astype(BF16)
    d_ord = dot_nt(d_ref[...], weight[:, :2304])
    d_h = dot_nt(d_ord.astype(BF16), choose_in[...])
    gain_grad[...] = jnp.broadcast_to(jnp.sum(d_h * unit, 0, keepdims=True), (8, 768))
    d_after = dy.astype(F32) + norm_back(d_h, gain, unit, scale)
    grad_after[...] = d_after
    low = d_after.astype(BF16)
    for target, part in halves:
        target[:, 2304:3072] = dot_tn(context[:, part], low).astype(BF16)


def attend_back_kernel(*refs):
    pieces = refs[:8]
    queries, key_values, prev, follow, grad_after, choose, cosine, sine = refs[8:16]
    grad_queries, grad_own, to_prev, to_follow, span, grads, d_ctx, weight, sems = refs[16:]
    copies = load_pieces(pieces, weight, sems, 2304)
    fill_span(span, prev, key_values, follow)
    low = grad_after[...].astype(BF16)
    wait_all(copies)
    d_ord = dot_nt(low, weight[...]).astype(BF16)
    d_ctx[...] = dot_nt(d_ord, choose[...]).astype(BF16)
    grads[...] = jnp.zeros_like(grads)
    cos_n, sin_n = cosine[...], sine[...]
    for block in range(2):
        bias = visible(span, block)
        rows = slice(block * 128, block * 128 + 128)
        cols = slice(block * 128, block * 128 + 256)
        for pair in range(6):
            lanes = slice(pair * 128, pair * 128 + 128)
            value_lanes = slice(768 + pair * 128, 768 + pair * 128 + 128)
            query_stack = head_stack(queries[rows, lanes])
            keys = span[cols, lanes]
            probs = probabilities(query_stack, keys, bias)
            d_stack = head_stack(d_ctx[rows, lanes])
            d_probs = dot_nt(d_stack, span[cols, value_lanes])
            delta = jnp.sum(d_probs * probs, -1, keepdims=True)
            d_scores = (probs * (d_probs - delta)).astype(BF16)
            d_query = head_merge(dot(d_scores, keys)) * 0.125
            grad_queries[rows, lanes] = rotate_back(
                d_query, cos_n[rows], sin_n[rows]
            ).astype(BF16)
            grads[cols, lanes] += dot_tn(d_scores, query_stack) * 0.125
            grads[cols, value_lanes] += dot_tn(probs.astype(BF16), d_stack)
    to_prev[...] = grads[:64].astype(BF16)
    to_follow[...] = grads[320:].astype(BF16)
    grad_own[...] = grads[64:320]


def project_back_kernel(*refs):
    pieces = refs[:8]
    (
        grad_queries,
        grad_own,
        from_prev,
        from_follow,
        tokens,
        gains,
        ordered,
        choose,
        cosine,
        sine,
        grad_after,
        gain_two_grad,
    ) = refs[8:20]
    input_grad, weight_own, *weight_other = refs[20:26]
    grad_kv, d_qkv, weight, sems = refs[26:]
    copies = load_pieces(pieces, weight, sems, 0)
    grad_kv[...] = grad_own[...]
    grad_kv[:64] += from_prev[...].astype(F32)
    grad_kv[192:] += from_follow[...].astype(F32)
    cos_w, sin_w = wide(cosine[...], 6), wide(sine[...], 6)
    d_qkv[:, :768] = grad_queries[...]
    d_qkv[:, 768:1536] = rotate_back(grad_kv[:, :768], cos_w, sin_w).astype(BF16)
    d_qkv[:, 1536:] = grad_kv[:, 768:].astype(BF16)
    grad = d_qkv[...]
    h_ord = ordered[...]
    weight_own[:, :2304] = dot_tn(h_ord[:, :384], grad).astype(BF16)
    far_grad = dot_tn(h_ord[:, 384:], grad).astype(BF16)
    for quarter, part in enumerate(weight_other):
        part[:, :2304] = far_grad[96 * quarter : 96 * quarter + 96]
    wait_all(copies)
    d_ord = dot_nt(grad, weight[:, :2304]).astype(BF16)
    d_h = dot_nt(d_ord, choose[...])
    unit, scale = normed(tokens[...].astype(F32))
    input_grad[...] = (grad_after[...] + norm_back(d_h, gains[0:1], unit, scale)).astype(BF16)
    first = jnp.sum(d_h * unit, 0, keepdims=True)
    row = lax.broadcasted_iota(jnp.int32, (8, 768), 0)
    both = jnp.where(row == 0, first, jnp.where(row == 1, gain_two_grad[0:1], 0.0))
    gain_order = dot(both.astype(BF16), choose[...]).astype(BF16)
    picks = unit_rows()
    weight_own[:, 2304:] = dot_tn(gain_order[:, :384], picks).astype(BF16)
    gain_cols = dot_tn(gain_order[:, 384:], picks).astype(BF16)
    for quarter, part in enumerate(weight_other):
        part[:, 2304:] = gain_cols[96 * quarter : 96 * quarter + 96]


def call(kernel, outs, pieces, args, flops, scratch):
    shapes = [jax.ShapeDtypeStruct(shape, dtype) for shape, dtype in outs]
    size = sum(v.size * v.dtype.itemsize for v in list(pieces) + list(args) + shapes)
    whole = pl.BlockSpec(memory_space=pltpu.VMEM)
    return pl.pallas_call(
        kernel,
        out_shape=shapes,
        in_specs=[pl.BlockSpec(memory_space=pl.ANY)] * len(pieces) + [whole] * len(args),
        out_specs=[whole] * len(outs),
        scratch_shapes=[pltpu.VMEM(shape, dtype) for shape, dtype in scratch]
        + [pltpu.SemaphoreType.DMA((8,))] * ((len(pieces) + 7) // 8),
        compiler_params=pltpu.CompilerParams(vmem_limit_bytes=48 * 1024 * 1024),
        cost_estimate=pl.CostEstimate(
            flops=int(flops), bytes_accessed=size if flops > 1 else 1, transcendentals=0
        ),
        name=kernel.__name__,
    )(*pieces, *args)


def small_call(kernel, shapes, args):
    whole = pl.BlockSpec(memory_space=pltpu.VMEM)
    return pl.pallas_call(
        kernel,
        out_shape=shapes,
        in_specs=[whole] * len(args),
        out_specs=jax.tree.map(lambda _: whole, shapes),
        compiler_params=pltpu.CompilerParams(vmem_limit_bytes=60 * 1024 * 1024),
        cost_estimate=pl.CostEstimate(flops=1, bytes_accessed=1, transcendentals=0),
        name=kernel.__name__,
    )(*args)


def pack_kernel(qkv, out, gate_up, down, gain_one, gain_two, packed):
    row = lax.broadcasted_iota(jnp.int32, (6, 6), 0)
    col = lax.broadcasted_iota(jnp.int32, (6, 6), 1)
    one = jnp.sum(jnp.where(row == col, gain_one[...].astype(F32), 0.0), 1, keepdims=True)
    two = jnp.sum(jnp.where(row == col, gain_two[...].astype(F32), 0.0), 1, keepdims=True)
    lane = lax.broadcasted_iota(jnp.int32, (6, 128), 1)
    gains = jnp.where(lane == 0, one, jnp.where(lane == 1, two, 0.0))
    packed[:, :2304] = qkv[...]
    packed[:, 2304:2432] = gains.astype(BF16)
    packed[:, 2432:4736] = gate_up[...]
    packed[:, 4736:5504] = out[...]
    rows = down[...].astype(F32)
    packed[:, 5504:6272] = rows[:6].astype(BF16)
    halves = []
    for index in range(6, 9):
        halves += [rows[index : index + 1, :384], rows[index : index + 1, 384:]]
    packed[:, 6272:] = jnp.concatenate(halves, 0).astype(BF16)


def stack_kernel(*refs):
    refs[-1][...] = jnp.concatenate([ref[...].astype(F32) for ref in refs[:-1]], 0).astype(BF16)


def fold_kernel(own, *refs):
    got, (mine, *parts) = refs[:-4], refs[-4:]
    size = mine.shape[0]
    for step, part in enumerate((mine, *parts)):
        rows = slice(step * size, (step + 1) * size)
        there = got[step][...] if len(got) == 4 else got[0][rows]
        part[...] = (own[rows].astype(F32) + there.astype(F32)).astype(part.dtype)


def fold(own, got):
    rows, cols = own.shape
    whole = pl.BlockSpec(memory_space=pltpu.VMEM)
    return pl.pallas_call(
        fold_kernel,
        out_shape=[jax.ShapeDtypeStruct((rows // 4, cols), F32)]
        + [jax.ShapeDtypeStruct((rows // 4, cols), BF16)] * 3,
        in_specs=[whole] * (1 + len(got)),
        out_specs=[whole] * 4,
        compiler_params=pltpu.CompilerParams(vmem_limit_bytes=48 * 1024 * 1024),
        cost_estimate=pl.CostEstimate(flops=1, bytes_accessed=1, transcendentals=0),
        name="fold_kernel",
    )(own, *got)


def line_total(mine, got):
    for part in got:
        mine = mine + part.astype(F32)
    return mine


def after_these(value, *others):
    return lax.optimization_barrier((value, others))[0]


def angle_tables(first):
    positions = (first + jnp.arange(256, dtype=jnp.int32)).astype(F32)
    freq_ids = jnp.arange(HEAD // 2, dtype=jnp.int32).astype(F32)
    inverse = jnp.exp(freq_ids * (-2.0 * math.log(10000.0) / HEAD))
    phases = positions[:, None] * inverse[None, :]
    return wide(jnp.cos(phases), 4), wide(jnp.sin(phases), 4)


def next_pairs(by):
    return [(i, i + by) for i in range(16) if 0 <= i + by < 16]


def body(
    tokens,
    segment_ids,
    norm_one,
    qkv_weight,
    out_weight,
    norm_two,
    in_weight,
    down_weight,
    cotangent,
):
    shard = small_call(
        pack_kernel,
        jax.ShapeDtypeStruct((6, 6656), BF16),
        (
            qkv_weight,
            out_weight,
            in_weight,
            down_weight,
            norm_one.reshape(1, 6),
            norm_two.reshape(1, 6),
        ),
    )
    slabs = line_gather(shard, "z")
    block_a = jnp.concatenate([v[:, :2432] for v in slabs], 0)
    block_b = jnp.concatenate([v[:, 2432:] for v in slabs], 0)
    block_a = jnp.concatenate(line_gather(block_a, "x"), 0)
    lines_b = line_gather(block_b, "y")
    block_a = after_these(block_a, lines_b)
    block_b = small_call(stack_kernel, jax.ShapeDtypeStruct((96, 4224), BF16), lines_b)
    lines_a = [block_a] + [line_send(block_a, "y", step) for step in (1, 2, 3)]
    pieces_a = lines_a + [swap_cores(v) for v in lines_a]
    near_b = [line_send(block_b, "x", step) for step in (2, 3)]
    far_b = line_send(after_these(block_b, near_b), "x", 1)
    natural_a, natural_b = after_these((owner_rows("y"), owner_rows("x")), block_a)
    choose_a = chooser(natural_a)
    choose_b = chooser(natural_b)
    choose_d = down_choosers(natural_b)

    inputs = tokens[0]
    marks = jnp.broadcast_to((segment_ids[0] + 1).astype(BF16)[:, None], (256, 128))
    place = (lax.axis_index("z") * 2 + lax.axis_index("x_hi")) * 2 + lax.axis_index("core")
    cosine, sine = angle_tables(place * 256)

    queries, key_values, ordered, gain_rows = call(
        project_kernel,
        [((256, 768), BF16), ((256, 1664), BF16), ((256, 768), BF16), ((8, 768), F32)],
        pieces_a,
        (
            after_these(inputs, choose_b, choose_d, near_b),
            choose_a,
            cosine,
            sine,
            marks,
        ),
        4e9,
        [((768, 2432), BF16)],
    )
    prev = lax.ppermute(key_values[192:], SEQ, next_pairs(1))
    follow = lax.ppermute(key_values[:64], SEQ, next_pairs(-1))
    far_b = after_these(far_b, prev, follow)
    block_b, near_b = after_these((block_b, near_b), gain_rows)
    lines_b = [block_b, far_b] + near_b
    pieces_b = lines_b + [swap_cores(v) for v in lines_b]
    context, after = call(
        attend_kernel,
        [((256, 768), BF16), ((256, 768), F32)],
        pieces_b,
        (queries, key_values, prev, follow, inputs, choose_b),
        4e9,
        [((384, 1664), BF16), ((256, 768), BF16), ((768, 768), BF16)],
    )
    mixed, rest_own, rest_other, grad_after, gain_two_grad = call(
        feed_kernel,
        [
            ((256, 768), BF16),
            ((384, 4224), BF16),
            ((384, 4224), BF16),
            ((256, 768), F32),
            ((8, 768), F32),
        ],
        pieces_b,
        (after, gain_rows, cotangent[0], context, choose_b) + choose_d,
        15e9,
        [((768, 4224), BF16), ((256, 2304), BF16)],
    )
    grad_queries, grad_kv, to_prev, to_follow = call(
        attend_back_kernel,
        [((256, 768), BF16), ((256, 1536), F32), ((64, 1536), BF16), ((64, 1536), BF16)],
        pieces_b,
        (queries, key_values, prev, follow, grad_after, choose_b, cosine, sine),
        10e9,
        [
            ((384, 1664), BF16),
            ((384, 1536), F32),
            ((256, 768), BF16),
            ((768, 768), BF16),
        ],
    )
    from_follow = lax.ppermute(to_prev, SEQ, next_pairs(-1))
    from_prev = lax.ppermute(to_follow, SEQ, next_pairs(1))
    rest_own = after_these(rest_own, grad_queries)
    rest_mine, *rest_parts = fold(rest_own, [swap_cores(rest_other)])
    rest_parts = after_these(rest_parts, from_prev, from_follow)
    rest_near = [line_send(part, "x", step) for step, part in zip((2, 3), rest_parts[1:])]
    rest_far = line_send(after_these(rest_parts[0], rest_near), "x", 1)
    input_grad, qkv_own, *qkv_other = call(
        project_back_kernel,
        [((256, 768), BF16), ((384, 2432), BF16)] + [((96, 2432), BF16)] * 4,
        pieces_a,
        (
            after_these(grad_queries, rest_parts),
            grad_kv,
            from_prev,
            from_follow,
            inputs,
            gain_rows,
            ordered,
            choose_a,
            cosine,
            sine,
            grad_after,
            gain_two_grad,
        ),
        1,
        [((256, 1536), F32), ((256, 2304), BF16), ((768, 2432), BF16)],
    )
    qkv_own = after_these(qkv_own, rest_near)
    qkv_mine, *qkv_parts = fold(qkv_own, [swap_cores(v) for v in qkv_other])
    qkv_lines = [line_send(part, "y", 4 - step) for step, part in zip((1, 2, 3), qkv_parts)]
    half_a = line_sum(line_total(qkv_mine, qkv_lines), "x")
    half_b = line_sum(line_total(rest_mine, rest_near + [rest_far]), "y")
    owned = line_sum(jnp.concatenate([half_a, half_b], 1), "z")
    owned_a, owned_b = owned[:, :2432], owned[:, 2432:]
    owned_down = jnp.concatenate([owned_b[:, 3072:3840], owned_b[:, 3840:].reshape(3, 768)], 0)
    return (
        mixed[None],
        input_grad[None],
        owned_a[:, 2304],
        owned_a[:, :2304],
        owned_b[:, 2304:3072],
        owned_a[:, 2305],
        owned_b[:, :2304],
        owned_down,
    )


def solution(mesh):
    fine = Mesh(mesh.devices.reshape(2, 4, 4, 2, 2), AXES)
    act = P(DP, SEQ, None)
    vec = P(AXES)
    mat = P(AXES, None)
    return jax.shard_map(
        body,
        mesh=fine,
        in_specs=(act, P(DP, SEQ), vec, mat, mat, vec, mat, mat, act),
        out_specs=(act, act, vec, mat, mat, vec, mat, mat),
        check_vma=False,
    )
```

profile of v0, /device:TPU:2, one launch (start us, length us, event | category | flops | bytes accessed | tf_op | source)
XLA Modules:
  0.0 222.4 jit_solution(1149385697553106077)
XLA Ops:
  2.2 4.0 %collective-permute-start.2 = (bf16[6,6656]{1,0:T(8,128)(2,1)}, bf16[6,6656]{1,0:T(8,128)(2,1)S(1)}, u32[]{:S(2)}, u32[]{:S(2)}) collective-permute-start(bf16[6,6656]{1,0:T(8,128)(2,1)} %pack_kernel.1), channel_id=1, source_target_pairs={{0,12},{4,0},{8,4},{12,8},{1,13},{5,1},{9,5},{13,9},{2,14},{6,2},{... | collective-permute-start | bytes 239624 | tf_op jit(solution)/shard_map/ppermute | solution.py:27
  11.1 2.5 %collective-permute-done.1 = bf16[6,6656]{1,0:T(8,128)(2,1)S(1)} collective-permute-done((bf16[6,6656]{1,0:T(8,128)(2,1)}, bf16[6,6656]{1,0:T(8,128)(2,1)S(1)}, u32[]{:S(2)}, u32[]{:S(2)}) %collective-permute-start.1) | collective-permute-done | bytes 79904 | tf_op jit(solution)/shard_map/ppermute | solution.py:27
  16.2 3.1 %collective-permute-start.5 = (bf16[24,4224]{1,0:T(8,128)(2,1)S(1)}, bf16[24,4224]{1,0:T(8,128)(2,1)S(1)}, u32[]{:S(2)}, u32[]{:S(2)}) collective-permute-start(bf16[24,4224]{1,0:T(8,128)(2,1)S(1)} %pad_maximum_fusion.1.refs_0_), channel_id=1, source_target_pairs={{0,48},{16,0},{32,16},{48,32},{1,49},{17,1},{33,17},{49,33},{2,50}... | collective-permute-start | bytes 608264 | tf_op jit(solution)/shard_map/ppermute | solution.py:27
  23.2 2.8 %collective-permute-done.9 = bf16[24,2432]{1,0:T(8,128)(2,1)S(1)} collective-permute-done((bf16[24,2432]{1,0:T(8,128)(2,1)S(1)}, bf16[24,2432]{1,0:T(8,128)(2,1)S(1)}, u32[]{:S(2)}, u32[]{:S(2)}) %collective-permute-start.9) | collective-permute-done | bytes 116768 | tf_op jit(solution)/shard_map/ppermute | solution.py:26
  26.0 3.0 %collective-permute-done.8 = bf16[24,2432]{1,0:T(8,128)(2,1)S(1)} collective-permute-done((bf16[24,2432]{1,0:T(8,128)(2,1)S(1)}, bf16[24,2432]{1,0:T(8,128)(2,1)S(1)}, u32[]{:S(2)}, u32[]{:S(2)}) %collective-permute-start.8) | collective-permute-done | bytes 116768 | tf_op jit(solution)/shard_map/ppermute | solution.py:26
  33.6 2.2 %stack_kernel.1.refs_0_ = bf16[96,4224]{1,0:T(8,128)(2,1)} custom-call(bf16[24,4224]{1,0:T(8,128)(2,1)} %copy-done.9, bf16[24,4224]{1,0:T(8,128)(2,1)} %copy-done.12, bf16[24,4224]{1,0:T(8,128)(2,1)} %copy-done.11, bf16[24,4224]{1,0:T(8,128)(2,1)} %copy-done.10), custom_call_target="tpu_custom_call" | custom-call | flops 1 | bytes 1 | tf_op jit(solution)/shard_map/stack_kernel/pallas_call | solution.py:378
  36.0 2.4 %collective-permute-start.6 = (bf16[96,4224]{1,0:T(8,128)(2,1)}, bf16[96,4224]{1,0:T(8,128)(2,1)S(1)}, u32[]{:S(2)}, u32[]{:S(2)}) collective-permute-start(bf16[96,4224]{1,0:T(8,128)(2,1)} %stack_kernel.1.refs_0_), channel_id=1, source_target_pairs={{0,64},{2,66},{64,0},{66,2},{1,65},{3,67},{65,1},{67,3},{4,68},{6,... | collective-permute-start | bytes 2433032 | tf_op jit(solution)/shard_map/ppermute | solution.py:26
  47.1 8.2 %collective-permute-done.11.refs_1_ = bf16[96,2432]{1,0:T(8,128)(2,1)S(1)} collective-permute-done((bf16[96,2432]{1,0:T(8,128)(2,1)S(1)}, bf16[96,2432]{1,0:T(8,128)(2,1)S(1)}, u32[]{:S(2)}, u32[]{:S(2)}) %collective-permute-start.11) | collective-permute-done | bytes 466976 | tf_op jit(solution)/shard_map/ppermute | solution.py:27
  59.8 6.3 %project_kernel.1 = (bf16[256,768]{1,0:T(8,128)(2,1)S(1)}, bf16[256,1664]{1,0:T(8,128)(2,1)S(1)}, bf16[256,768]{1,0:T(8,128)(2,1)S(1)}, f32[8,768]{1,0:T(8,128)S(1)}) custom-call(bf16[96,2432]{1,0:T(8,128)(2,1)S(1)} %concatenate.24.refs_0_, bf16[96,2432]{1,0:T(8,128)(2,1)S(1)} %collective-permute-done.11.refs_1_, ...), custom_call_target="tpu_custom_call" | custom-call | flops 4000000000 | bytes 7299072 | tf_op jit(solution)/shard_map/project_kernel/pallas_call | solution.py:361
  67.5 3.0 %collective-permute-start.19 = (bf16[64,1664]{1,0:T(8,128)(2,1)S(1)}, bf16[64,1664]{1,0:T(8,128)(2,1)S(1)}, u32[]{:S(2)}, u32[]{:S(2)}) collective-permute-start(bf16[64,1664]{1,0:T(8,128)(2,1)S(1)} %get-tuple-element.105), channel_id=1, source_target_pairs={{0,1},{1,2},{2,3},{3,4},{4,5},{5,6},{6,7},{7,8},{8,9},{9,10},{10,1... | collective-permute-start | bytes 638984 | tf_op jit(solution)/shard_map/ppermute | solution.py:516
  70.6 3.0 %collective-permute-start.21 = (bf16[96,4224]{1,0:T(8,128)(2,1)S(1)}, bf16[96,4224]{1,0:T(8,128)(2,1)S(1)}, u32[]{:S(2)}, u32[]{:S(2)}) collective-permute-start(bf16[96,4224]{1,0:T(8,128)(2,1)S(1)} %copy-done.1), channel_id=1, source_target_pairs={{0,1},{1,0},{2,3},{3,2},{4,5},{5,4},{6,7},{7,6},{8,9},{9,8},{10,11... | collective-permute-start | bytes 2433032 | tf_op jit(solution)/shard_map/ppermute | solution.py:21
  73.7 10.2 %collective-permute-start.24 = (bf16[96,4224]{1,0:T(8,128)(2,1)S(1)}, bf16[96,4224]{1,0:T(8,128)(2,1)S(1)}, u32[]{:S(2)}, u32[]{:S(2)}) collective-permute-start(bf16[96,4224]{1,0:T(8,128)(2,1)S(1)} %collective-permute-done.7.refs_3_), channel_id=1, source_target_pairs={{0,1},{1,0},{2,3},{3,2},{4,5},{5,4},{6,7},{7,6},{8,9},{9,8},{10,11... | collective-permute-start | bytes 2433032 | tf_op jit(solution)/shard_map/ppermute | solution.py:21
  87.9 5.2 %attend_kernel.1 = (bf16[256,768]{1,0:T(8,128)(2,1)S(1)}, f32[256,768]{1,0:T(8,128)S(1)}) custom-call(bf16[96,4224]{1,0:T(8,128)(2,1)S(1)} %copy-done.1, bf16[96,4224]{1,0:T(8,128)(2,1)S(1)} %collective-permute-done.18.refs_1_, bf16[96,4224]{1,0:T(8,128)(2,1)S(1)} %collective-permute-done.6.refs_2_, bf16[96,4224]{1,0:T(8,128)(2,1)S(1)} %collective-permute-done.7.refs_3_, ...), custom_call_target="tpu_custom_call" | custom-call | flops 4000000000 | bytes 10911744 | tf_op jit(solution)/shard_map/attend_kernel/pallas_call | solution.py:361
  93.1 18.0 %feed_kernel.1 = (bf16[256,768]{1,0:T(8,128)(2,1)}, bf16[384,4224]{1,0:T(8,128)(2,1)}, bf16[384,4224]{1,0:T(8,128)(2,1)}, f32[256,768]{1,0:T(8,128)S(1)}, f32[8,768]{1,0:T(8,128)S(1)}) custom-call(bf16[96,4224]{1,0:T(8,128)(2,1)S(1)} %copy-done.1, bf16[96,4224]{1,0:T(8,128)(2,1)S(1)} %collective-permute-done.18.refs_1_, ...), custom_call_target="tpu_custom_call" | custom-call | flops 15000000512 | bytes 22265856 | tf_op jit(solution)/shard_map/feed_kernel/pallas_call | solution.py:361
  111.2 9.3 %collective-permute-start.25 = (bf16[384,4224]{1,0:T(8,128)(2,1)}, bf16[384,4224]{1,0:T(8,128)(2,1)}, u32[]{:S(2)}, u32[]{:S(2)}) collective-permute-start(bf16[384,4224]{1,0:T(8,128)(2,1)} %get-tuple-element.72), channel_id=1, source_target_pairs={{0,1},{1,0},{2,3},{3,2},{4,5},{5,4},{6,7},{7,6},{8,9},{9,8},{10,11... | collective-permute-start | bytes 9732104 | tf_op jit(solution)/shard_map/ppermute | solution.py:21
  120.4 11.6 %attend_back_kernel.1 = (bf16[256,768]{1,0:T(8,128)(2,1)S(1)}, f32[256,1536]{1,0:T(8,128)}, bf16[64,1536]{1,0:T(8,128)(2,1)S(1)}, bf16[64,1536]{1,0:T(8,128)(2,1)S(1)}) custom-call(bf16[96,4224]{1,0:T(8,128)(2,1)S(1)} %copy-done.1, bf16[96,4224]{1,0:T(8,128)(2,1)S(1)} %collective-permute-done.18.refs_1_, ...), custom_call_target="tpu_custom_call" | custom-call | flops 10000000000 | bytes 12746752 | tf_op jit(solution)/shard_map/attend_back_kernel/pallas_call | solution.py:361
  132.0 2.1 collective-permute-start.26
  135.4 3.6 %fold_kernel.2 = (f32[96,4224]{1,0:T(8,128)S(1)}, bf16[96,4224]{1,0:T(8,128)(2,1)S(1)}, bf16[96,4224]{1,0:T(8,128)(2,1)S(1)}, bf16[96,4224]{1,0:T(8,128)(2,1)S(1)}) custom-call(bf16[384,4224]{1,0:T(8,128)(2,1)} %get-tuple-element.71.own, bf16[384,4224]{1,0:T(8,128)(2,1)} %collective-permute-done.25.refs_0_), custom_call_target="tpu_custom_call" | custom-call | flops 1 | bytes 1 | tf_op jit(solution)/shard_map/fold_kernel/pallas_call | solution.py:424
  139.0 2.9 %collective-permute-start.28 = (bf16[96,4224]{1,0:T(8,128)(2,1)S(1)}, bf16[96,4224]{1,0:T(8,128)(2,1)S(1)}, u32[]{:S(2)}, u32[]{:S(2)}) collective-permute-start(bf16[96,4224]{1,0:T(8,128)(2,1)S(1)} %get-tuple-element.79), channel_id=1, source_target_pairs={{0,64},{2,66},{64,0},{66,2},{1,65},{3,67},{65,1},{67,3},{4,68},{6,... | collective-permute-start | bytes 2433032 | tf_op jit(solution)/shard_map/ppermute | solution.py:26
  143.7 9.5 %project_back_kernel.1 = (bf16[256,768]{1,0:T(8,128)(2,1)}, bf16[384,2432]{1,0:T(8,128)(2,1)}, bf16[96,2432]{1,0:T(8,128)(2,1)S(1)}, bf16[96,2432]{1,0:T(8,128)(...) custom-call(bf16[96,2432]{1,0:T(8,128)(2,1)S(1)} %concatenate.24.refs_0_, ...), custom_call_target="tpu_custom_call" | custom-call | flops 1 | bytes 1 | tf_op jit(solution)/shard_map/project_back_kernel/pallas_call | solution.py:361
  153.2 3.5 %collective-permute-start.30 = (bf16[96,2432]{1,0:T(8,128)(2,1)S(1)}, bf16[96,2432]{1,0:T(8,128)(2,1)S(1)}, u32[]{:S(2)}, u32[]{:S(2)}) collective-permute-start(bf16[96,2432]{1,0:T(8,128)(2,1)S(1)} %get-tuple-element.88), channel_id=1, source_target_pairs={{0,1},{1,0},{2,3},{3,2},{4,5},{5,4},{6,7},{7,6},{8,9},{9,8},{10,11... | collective-permute-start | bytes 1400840 | tf_op jit(solution)/shard_map/ppermute | solution.py:21
  158.0 2.7 %collective-permute-start.33 = (bf16[96,2432]{1,0:T(8,128)(2,1)S(1)}, bf16[96,2432]{1,0:T(8,128)(2,1)S(1)}, u32[]{:S(2)}, u32[]{:S(2)}) collective-permute-start(bf16[96,2432]{1,0:T(8,128)(2,1)S(1)} %get-tuple-element.91), channel_id=1, source_target_pairs={{0,1},{1,0},{2,3},{3,2},{4,5},{5,4},{6,7},{7,6},{8,9},{9,8},{10,11... | collective-permute-start | bytes 1400840 | tf_op jit(solution)/shard_map/ppermute | solution.py:21
  164.1 2.8 %collective-permute-start.34 = (bf16[96,2432]{1,0:T(8,128)(2,1)S(1)}, bf16[96,2432]{1,0:T(8,128)(2,1)S(1)}, u32[]{:S(2)}, u32[]{:S(2)}) collective-permute-start(bf16[96,2432]{1,0:T(8,128)(2,1)S(1)} %get-tuple-element.93), channel_id=1, source_target_pairs={{0,48},{16,0},{32,16},{48,32},{1,49},{17,1},{33,17},{49,33},{2,50}... | collective-permute-start | bytes 1400840 | tf_op jit(solution)/shard_map/ppermute | solution.py:27
  169.4 3.4 %collective-permute-start.40 = (bf16[96,4224]{1,0:T(8,128)(2,1)S(1)}, bf16[96,4224]{1,0:T(8,128)(2,1)S(1)}, u32[]{:S(2)}, u32[]{:S(2)}) collective-permute-start(bf16[96,4224]{1,0:T(8,128)(2,1)S(1)} %get-tuple-element.97), channel_id=1, source_target_pairs={{0,2},{2,0},{64,66},{66,64},{1,3},{3,1},{65,67},{67,65},{4,6},{6,4... | collective-permute-start | bytes 2433032 | tf_op jit(solution)/shard_map/ppermute | solution.py:26
  172.8 14.7 %collective-permute-done.34 = bf16[96,2432]{1,0:T(8,128)(2,1)S(1)} collective-permute-done((bf16[96,2432]{1,0:T(8,128)(2,1)S(1)}, bf16[96,2432]{1,0:T(8,128)(2,1)S(1)}, u32[]{:S(2)}, u32[]{:S(2)}) %collective-permute-start.34) | collective-permute-done | bytes 466976 | tf_op jit(solution)/shard_map/ppermute | solution.py:27
  187.6 3.7 %collective-permute-done.36 = bf16[96,2432]{1,0:T(8,128)(2,1)S(1)} collective-permute-done((bf16[96,2432]{1,0:T(8,128)(2,1)S(1)}, bf16[96,2432]{1,0:T(8,128)(2,1)S(1)}, u32[]{:S(2)}, u32[]{:S(2)}) %collective-permute-start.36) | collective-permute-done | bytes 466976 | tf_op jit(solution)/shard_map/ppermute | solution.py:27
  191.5 4.2 %collective-permute-start.37 = (bf16[24,2432]{1,0:T(8,128)(2,1)S(1)}, bf16[24,2432]{1,0:T(8,128)(2,1)S(1)}, u32[]{:S(2)}, u32[]{:S(2)}) collective-permute-start(bf16[24,2432]{1,0:T(8,128)(2,1)S(1)} %get-tuple-element.109), channel_id=1, source_target_pairs={{0,2},{2,0},{64,66},{66,64},{1,3},{3,1},{65,67},{67,65},{4,6},{6,4... | collective-permute-start | bytes 350216 | tf_op jit(solution)/shard_map/ppermute | solution.py:26
  202.9 2.8 %collective-permute-done.41 = bf16[24,4224]{1,0:T(8,128)(2,1)S(1)} collective-permute-done((bf16[24,4224]{1,0:T(8,128)(2,1)S(1)}, bf16[24,4224]{1,0:T(8,128)(2,1)S(1)}, u32[]{:S(2)}, u32[]{:S(2)}) %collective-permute-start.41) | collective-permute-done | bytes 202784 | tf_op jit(solution)/shard_map/ppermute | solution.py:27
  205.7 4.2 %collective-permute-done.43 = bf16[24,4224]{1,0:T(8,128)(2,1)S(1)} collective-permute-done((bf16[24,4224]{1,0:T(8,128)(2,1)S(1)}, bf16[24,4224]{1,0:T(8,128)(2,1)S(1)}, u32[]{:S(2)}, u32[]{:S(2)}) %collective-permute-start.43) | collective-permute-done | bytes 202784 | tf_op jit(solution)/shard_map/ppermute | solution.py:27
  210.1 2.3 %collective-permute-start.44 = (bf16[6,6656]{1,0:T(8,128)(2,1)S(1)}, bf16[6,6656]{1,0:T(8,128)(2,1)S(1)}, u32[]{:S(2)}, u32[]{:S(2)}) collective-permute-start(bf16[6,6656]{1,0:T(8,128)(2,1)S(1)} %get-tuple-element.112), channel_id=1, source_target_pairs={{0,12},{4,0},{8,4},{12,8},{1,13},{5,1},{9,5},{13,9},{2,14},{6,2},{... | collective-permute-start | bytes 239624 | tf_op jit(solution)/shard_map/ppermute | solution.py:27
  212.4 3.1 %collective-permute-start.45 = (bf16[6,6656]{1,0:T(8,128)(2,1)S(1)}, bf16[6,6656]{1,0:T(8,128)(2,1)S(1)}, u32[]{:S(2)}, u32[]{:S(2)}) collective-permute-start(bf16[6,6656]{1,0:T(8,128)(2,1)S(1)} %get-tuple-element.114), channel_id=1, source_target_pairs={{0,8},{4,12},{8,0},{12,4},{1,9},{5,13},{9,1},{13,5},{2,10},{6,14},... | collective-permute-start | bytes 239624 | tf_op jit(solution)/shard_map/ppermute | solution.py:27
  215.7 3.7 %collective-permute-done.46 = bf16[6,6656]{1,0:T(8,128)(2,1)S(1)} collective-permute-done((bf16[6,6656]{1,0:T(8,128)(2,1)S(1)}, bf16[6,6656]{1,0:T(8,128)(2,1)S(1)}, u32[]{:S(2)}, u32[]{:S(2)}) %collective-permute-start.46) | collective-permute-done | bytes 79904 | tf_op jit(solution)/shard_map/ppermute | solution.py:27
  (147 shorter events, 57.0 us)
Async XLA Ops:
  2.2 8.9 %collective-permute-start.2 = (bf16[6,6656]{1,0:T(8,128)(2,1)}, bf16[6,6656]{1,0:T(8,128)(2,1)S(1)}, u32[]{:S(2)}, u32[]{:S(2)}) collective-permute-start(bf16[6,6656]{1,0:T(8,128)(2,1)} %pack_kernel.1), channel_id=1, source_target_pairs={{0,12},{4,0},{8,4},{12,8},{1,13},{5,1},{9,5},{13,9},{2,14},{6,2},{... | collective-permute-start | bytes 239624 | tf_op jit(solution)/shard_map/ppermute | solution.py:27
  6.2 7.4 %collective-permute-start.1 = (bf16[6,6656]{1,0:T(8,128)(2,1)}, bf16[6,6656]{1,0:T(8,128)(2,1)S(1)}, u32[]{:S(2)}, u32[]{:S(2)}) collective-permute-start(bf16[6,6656]{1,0:T(8,128)(2,1)} %pack_kernel.1), channel_id=1, source_target_pairs={{0,8},{4,12},{8,0},{12,4},{1,9},{5,13},{9,1},{13,5},{2,10},{6,14},... | collective-permute-start | bytes 239624 | tf_op jit(solution)/shard_map/ppermute | solution.py:27
  6.2 8.1 %collective-permute-start = (bf16[6,6656]{1,0:T(8,128)(2,1)}, bf16[6,6656]{1,0:T(8,128)(2,1)S(1)}, u32[]{:S(2)}, u32[]{:S(2)}) collective-permute-start(bf16[6,6656]{1,0:T(8,128)(2,1)} %pack_kernel.1), channel_id=1, source_target_pairs={{0,4},{4,8},{8,12},{12,0},{1,5},{5,9},{9,13},{13,1},{2,6},{6,10},{... | collective-permute-start | bytes 239624 | tf_op jit(solution)/shard_map/ppermute | solution.py:27
  14.4 8.3 %collective-permute-start.10 = (bf16[24,2432]{1,0:T(8,128)(2,1)S(1)}, bf16[24,2432]{1,0:T(8,128)(2,1)S(1)}, u32[]{:S(2)}, u32[]{:S(2)}) collective-permute-start(bf16[24,2432]{1,0:T(8,128)(2,1)S(1)} %pad_maximum_fusion.4), channel_id=1, source_target_pairs={{0,66},{2,64},{64,2},{66,0},{1,67},{3,65},{65,3},{67,1},{4,70},{6,... | collective-permute-start | bytes 350216 | tf_op jit(solution)/shard_map/ppermute | solution.py:26
  16.2 13.4 %collective-permute-start.5 = (bf16[24,4224]{1,0:T(8,128)(2,1)S(1)}, bf16[24,4224]{1,0:T(8,128)(2,1)S(1)}, u32[]{:S(2)}, u32[]{:S(2)}) collective-permute-start(bf16[24,4224]{1,0:T(8,128)(2,1)S(1)} %pad_maximum_fusion.1.refs_0_), channel_id=1, source_target_pairs={{0,48},{16,0},{32,16},{48,32},{1,49},{17,1},{33,17},{49,33},{2,50}... | collective-permute-start | bytes 608264 | tf_op jit(solution)/shard_map/ppermute | solution.py:27
  19.3 10.3 %collective-permute-start.4 = (bf16[24,4224]{1,0:T(8,128)(2,1)S(1)}, bf16[24,4224]{1,0:T(8,128)(2,1)S(1)}, u32[]{:S(2)}, u32[]{:S(2)}) collective-permute-start(bf16[24,4224]{1,0:T(8,128)(2,1)S(1)} %pad_maximum_fusion.1.refs_0_), channel_id=1, source_target_pairs={{0,32},{16,48},{32,0},{48,16},{1,33},{17,49},{33,1},{49,17},{2,34}... | collective-permute-start | bytes 608264 | tf_op jit(solution)/shard_map/ppermute | solution.py:27
  19.9 11.3 %collective-permute-start.3 = (bf16[24,4224]{1,0:T(8,128)(2,1)S(1)}, bf16[24,4224]{1,0:T(8,128)(2,1)S(1)}, u32[]{:S(2)}, u32[]{:S(2)}) collective-permute-start(bf16[24,4224]{1,0:T(8,128)(2,1)S(1)} %pad_maximum_fusion.1.refs_0_), channel_id=1, source_target_pairs={{0,16},{16,32},{32,48},{48,0},{1,17},{17,33},{33,49},{49,1},{2,18}... | collective-permute-start | bytes 608264 | tf_op jit(solution)/shard_map/ppermute | solution.py:27
  31.2 14.1 %collective-permute-start.13 = (bf16[96,2432]{1,0:T(8,128)(2,1)S(1)}, bf16[96,2432]{1,0:T(8,128)(2,1)S(1)}, u32[]{:S(2)}, u32[]{:S(2)}) collective-permute-start(bf16[96,2432]{1,0:T(8,128)(2,1)S(1)} %concatenate.24.refs_0_), channel_id=1, source_target_pairs={{0,48},{16,0},{32,16},{48,32},{1,49},{17,1},{33,17},{49,33},{2,50}... | collective-permute-start | bytes 1400840 | tf_op jit(solution)/shard_map/ppermute | solution.py:27
  31.9 15.2 %collective-permute-start.12 = (bf16[96,2432]{1,0:T(8,128)(2,1)S(1)}, bf16[96,2432]{1,0:T(8,128)(2,1)S(1)}, u32[]{:S(2)}, u32[]{:S(2)}) collective-permute-start(bf16[96,2432]{1,0:T(8,128)(2,1)S(1)} %concatenate.24.refs_0_), channel_id=1, source_target_pairs={{0,32},{16,48},{32,0},{48,16},{1,33},{17,49},{33,1},{49,17},{2,34}... | collective-permute-start | bytes 1400840 | tf_op jit(solution)/shard_map/ppermute | solution.py:27
  33.6 21.7 %collective-permute-start.11 = (bf16[96,2432]{1,0:T(8,128)(2,1)S(1)}, bf16[96,2432]{1,0:T(8,128)(2,1)S(1)}, u32[]{:S(2)}, u32[]{:S(2)}) collective-permute-start(bf16[96,2432]{1,0:T(8,128)(2,1)S(1)} %concatenate.24.refs_0_), channel_id=1, source_target_pairs={{0,16},{16,32},{32,48},{48,0},{1,17},{17,33},{33,49},{49,1},{2,18}... | collective-permute-start | bytes 1400840 | tf_op jit(solution)/shard_map/ppermute | solution.py:27
  35.9 19.4 %collective-permute-start.7 = (bf16[96,4224]{1,0:T(8,128)(2,1)}, bf16[96,4224]{1,0:T(8,128)(2,1)S(1)}, u32[]{:S(2)}, u32[]{:S(2)}) collective-permute-start(bf16[96,4224]{1,0:T(8,128)(2,1)} %stack_kernel.1.refs_0_), channel_id=1, source_target_pairs={{0,66},{2,64},{64,2},{66,0},{1,67},{3,65},{65,3},{67,1},{4,70},{6,... | collective-permute-start | bytes 2433032 | tf_op jit(solution)/shard_map/ppermute | solution.py:26
  36.0 21.8 %collective-permute-start.6 = (bf16[96,4224]{1,0:T(8,128)(2,1)}, bf16[96,4224]{1,0:T(8,128)(2,1)S(1)}, u32[]{:S(2)}, u32[]{:S(2)}) collective-permute-start(bf16[96,4224]{1,0:T(8,128)(2,1)} %stack_kernel.1.refs_0_), channel_id=1, source_target_pairs={{0,64},{2,66},{64,0},{66,2},{1,65},{3,67},{65,1},{67,3},{4,68},{6,... | collective-permute-start | bytes 2433032 | tf_op jit(solution)/shard_map/ppermute | solution.py:26
  45.2 14.4 %collective-permute-start.14 = (bf16[96,2432]{1,0:T(8,128)(2,1)S(1)}, bf16[96,2432]{1,0:T(8,128)(2,1)S(1)}, u32[]{:S(2)}, u32[]{:S(2)}) collective-permute-start(bf16[96,2432]{1,0:T(8,128)(2,1)S(1)} %concatenate.24.refs_0_), channel_id=1, source_target_pairs={{0,1},{1,0},{2,3},{3,2},{4,5},{5,4},{6,7},{7,6},{8,9},{9,8},{10,11... | collective-permute-start | bytes 1400840 | tf_op jit(solution)/shard_map/ppermute | solution.py:21
  47.1 12.5 %collective-permute-start.17 = (bf16[96,2432]{1,0:T(8,128)(2,1)S(1)}, bf16[96,2432]{1,0:T(8,128)(2,1)S(1)}, u32[]{:S(2)}, u32[]{:S(2)}) collective-permute-start(bf16[96,2432]{1,0:T(8,128)(2,1)S(1)} %collective-permute-done.13.refs_3_), channel_id=1, source_target_pairs={{0,1},{1,0},{2,3},{3,2},{4,5},{5,4},{6,7},{7,6},{8,9},{9,8},{10,11... | collective-permute-start | bytes 1400840 | tf_op jit(solution)/shard_map/ppermute | solution.py:21
  57.8 26.1 %collective-permute-start.18 = (bf16[96,4224]{1,0:T(8,128)(2,1)S(1)}, bf16[96,4224]{1,0:T(8,128)(2,1)S(1)}, u32[]{:S(2)}, u32[]{:S(2)}) collective-permute-start(bf16[96,4224]{1,0:T(8,128)(2,1)S(1)} %copy-done.1), channel_id=1, source_target_pairs={{0,2},{2,0},{64,66},{66,64},{1,3},{3,1},{65,67},{67,65},{4,6},{6,4... | collective-permute-start | bytes 2433032 | tf_op jit(solution)/shard_map/ppermute | solution.py:26
  66.2 7.5 %collective-permute-start.20 = (bf16[64,1664]{1,0:T(8,128)(2,1)S(1)}, bf16[64,1664]{1,0:T(8,128)(2,1)S(1)}, u32[]{:S(2)}, u32[]{:S(2)}) collective-permute-start(bf16[64,1664]{1,0:T(8,128)(2,1)S(1)} %get-tuple-element.104), channel_id=1, source_target_pairs={{1,0},{2,1},{3,2},{4,3},{5,4},{6,5},{7,6},{8,7},{9,8},{10,9},{11,1... | collective-permute-start | bytes 638984 | tf_op jit(solution)/shard_map/ppermute | solution.py:517
  67.5 16.4 %collective-permute-start.19 = (bf16[64,1664]{1,0:T(8,128)(2,1)S(1)}, bf16[64,1664]{1,0:T(8,128)(2,1)S(1)}, u32[]{:S(2)}, u32[]{:S(2)}) collective-permute-start(bf16[64,1664]{1,0:T(8,128)(2,1)S(1)} %get-tuple-element.105), channel_id=1, source_target_pairs={{0,1},{1,2},{2,3},{3,4},{4,5},{5,6},{6,7},{7,8},{8,9},{9,10},{10,1... | collective-permute-start | bytes 638984 | tf_op jit(solution)/shard_map/ppermute | solution.py:516
  70.6 13.4 %collective-permute-start.21 = (bf16[96,4224]{1,0:T(8,128)(2,1)S(1)}, bf16[96,4224]{1,0:T(8,128)(2,1)S(1)}, u32[]{:S(2)}, u32[]{:S(2)}) collective-permute-start(bf16[96,4224]{1,0:T(8,128)(2,1)S(1)} %copy-done.1), channel_id=1, source_target_pairs={{0,1},{1,0},{2,3},{3,2},{4,5},{5,4},{6,7},{7,6},{8,9},{9,8},{10,11... | collective-permute-start | bytes 2433032 | tf_op jit(solution)/shard_map/ppermute | solution.py:21
  73.6 10.4 %collective-permute-start.23 = (bf16[96,4224]{1,0:T(8,128)(2,1)S(1)}, bf16[96,4224]{1,0:T(8,128)(2,1)S(1)}, u32[]{:S(2)}, u32[]{:S(2)}) collective-permute-start(bf16[96,4224]{1,0:T(8,128)(2,1)S(1)} %collective-permute-done.6.refs_2_), channel_id=1, source_target_pairs={{0,1},{1,0},{2,3},{3,2},{4,5},{5,4},{6,7},{7,6},{8,9},{9,8},{10,11... | collective-permute-start | bytes 2433032 | tf_op jit(solution)/shard_map/ppermute | solution.py:21
  73.7 12.2 %collective-permute-start.24 = (bf16[96,4224]{1,0:T(8,128)(2,1)S(1)}, bf16[96,4224]{1,0:T(8,128)(2,1)S(1)}, u32[]{:S(2)}, u32[]{:S(2)}) collective-permute-start(bf16[96,4224]{1,0:T(8,128)(2,1)S(1)} %collective-permute-done.7.refs_3_), channel_id=1, source_target_pairs={{0,1},{1,0},{2,3},{3,2},{4,5},{5,4},{6,7},{7,6},{8,9},{9,8},{10,11... | collective-permute-start | bytes 2433032 | tf_op jit(solution)/shard_map/ppermute | solution.py:21
  111.2 24.2 %collective-permute-start.25 = (bf16[384,4224]{1,0:T(8,128)(2,1)}, bf16[384,4224]{1,0:T(8,128)(2,1)}, u32[]{:S(2)}, u32[]{:S(2)}) collective-permute-start(bf16[384,4224]{1,0:T(8,128)(2,1)} %get-tuple-element.72), channel_id=1, source_target_pairs={{0,1},{1,0},{2,3},{3,2},{4,5},{5,4},{6,7},{7,6},{8,9},{9,8},{10,11... | collective-permute-start | bytes 9732104 | tf_op jit(solution)/shard_map/ppermute | solution.py:21
  139.0 18.9 %collective-permute-start.28 = (bf16[96,4224]{1,0:T(8,128)(2,1)S(1)}, bf16[96,4224]{1,0:T(8,128)(2,1)S(1)}, u32[]{:S(2)}, u32[]{:S(2)}) collective-permute-start(bf16[96,4224]{1,0:T(8,128)(2,1)S(1)} %get-tuple-element.79), channel_id=1, source_target_pairs={{0,64},{2,66},{64,0},{66,2},{1,65},{3,67},{65,1},{67,3},{4,68},{6,... | collective-permute-start | bytes 2433032 | tf_op jit(solution)/shard_map/ppermute | solution.py:26
  141.9 18.7 %collective-permute-start.29 = (bf16[96,4224]{1,0:T(8,128)(2,1)S(1)}, bf16[96,4224]{1,0:T(8,128)(2,1)S(1)}, u32[]{:S(2)}, u32[]{:S(2)}) collective-permute-start(bf16[96,4224]{1,0:T(8,128)(2,1)S(1)} %get-tuple-element.80), channel_id=1, source_target_pairs={{0,66},{2,64},{64,2},{66,0},{1,67},{3,65},{65,3},{67,1},{4,70},{6,... | collective-permute-start | bytes 2433032 | tf_op jit(solution)/shard_map/ppermute | solution.py:26
  153.2 7.4 %collective-permute-start.30 = (bf16[96,2432]{1,0:T(8,128)(2,1)S(1)}, bf16[96,2432]{1,0:T(8,128)(2,1)S(1)}, u32[]{:S(2)}, u32[]{:S(2)}) collective-permute-start(bf16[96,2432]{1,0:T(8,128)(2,1)S(1)} %get-tuple-element.88), channel_id=1, source_target_pairs={{0,1},{1,0},{2,3},{3,2},{4,5},{5,4},{6,7},{7,6},{8,9},{9,8},{10,11... | collective-permute-start | bytes 1400840 | tf_op jit(solution)/shard_map/ppermute | solution.py:21
  164.1 23.5 %collective-permute-start.34 = (bf16[96,2432]{1,0:T(8,128)(2,1)S(1)}, bf16[96,2432]{1,0:T(8,128)(2,1)S(1)}, u32[]{:S(2)}, u32[]{:S(2)}) collective-permute-start(bf16[96,2432]{1,0:T(8,128)(2,1)S(1)} %get-tuple-element.93), channel_id=1, source_target_pairs={{0,48},{16,0},{32,16},{48,32},{1,49},{17,1},{33,17},{49,33},{2,50}... | collective-permute-start | bytes 1400840 | tf_op jit(solution)/shard_map/ppermute | solution.py:27
  166.8 20.8 %collective-permute-start.35 = (bf16[96,2432]{1,0:T(8,128)(2,1)S(1)}, bf16[96,2432]{1,0:T(8,128)(2,1)S(1)}, u32[]{:S(2)}, u32[]{:S(2)}) collective-permute-start(bf16[96,2432]{1,0:T(8,128)(2,1)S(1)} %get-tuple-element.94), channel_id=1, source_target_pairs={{0,32},{16,48},{32,0},{48,16},{1,33},{17,49},{33,1},{49,17},{2,34}... | collective-permute-start | bytes 1400840 | tf_op jit(solution)/shard_map/ppermute | solution.py:27
  168.1 23.2 %collective-permute-start.36 = (bf16[96,2432]{1,0:T(8,128)(2,1)S(1)}, bf16[96,2432]{1,0:T(8,128)(2,1)S(1)}, u32[]{:S(2)}, u32[]{:S(2)}) collective-permute-start(bf16[96,2432]{1,0:T(8,128)(2,1)S(1)} %get-tuple-element.95), channel_id=1, source_target_pairs={{0,16},{16,32},{32,48},{48,0},{1,17},{17,33},{33,49},{49,1},{2,18}... | collective-permute-start | bytes 1400840 | tf_op jit(solution)/shard_map/ppermute | solution.py:27
  169.4 27.8 %collective-permute-start.40 = (bf16[96,4224]{1,0:T(8,128)(2,1)S(1)}, bf16[96,4224]{1,0:T(8,128)(2,1)S(1)}, u32[]{:S(2)}, u32[]{:S(2)}) collective-permute-start(bf16[96,4224]{1,0:T(8,128)(2,1)S(1)} %get-tuple-element.97), channel_id=1, source_target_pairs={{0,2},{2,0},{64,66},{66,64},{1,3},{3,1},{65,67},{67,65},{4,6},{6,4... | collective-permute-start | bytes 2433032 | tf_op jit(solution)/shard_map/ppermute | solution.py:26
  191.5 8.2 %collective-permute-start.37 = (bf16[24,2432]{1,0:T(8,128)(2,1)S(1)}, bf16[24,2432]{1,0:T(8,128)(2,1)S(1)}, u32[]{:S(2)}, u32[]{:S(2)}) collective-permute-start(bf16[24,2432]{1,0:T(8,128)(2,1)S(1)} %get-tuple-element.109), channel_id=1, source_target_pairs={{0,2},{2,0},{64,66},{66,64},{1,3},{3,1},{65,67},{67,65},{4,6},{6,4... | collective-permute-start | bytes 350216 | tf_op jit(solution)/shard_map/ppermute | solution.py:26
  197.6 8.0 %collective-permute-start.41 = (bf16[24,4224]{1,0:T(8,128)(2,1)S(1)}, bf16[24,4224]{1,0:T(8,128)(2,1)S(1)}, u32[]{:S(2)}, u32[]{:S(2)}) collective-permute-start(bf16[24,4224]{1,0:T(8,128)(2,1)S(1)} %get-tuple-element.106), channel_id=1, source_target_pairs={{0,48},{16,0},{32,16},{48,32},{1,49},{17,1},{33,17},{49,33},{2,50}... | collective-permute-start | bytes 608264 | tf_op jit(solution)/shard_map/ppermute | solution.py:27
  198.3 11.6 %collective-permute-start.43 = (bf16[24,4224]{1,0:T(8,128)(2,1)S(1)}, bf16[24,4224]{1,0:T(8,128)(2,1)S(1)}, u32[]{:S(2)}, u32[]{:S(2)}) collective-permute-start(bf16[24,4224]{1,0:T(8,128)(2,1)S(1)} %get-tuple-element.107), channel_id=1, source_target_pairs={{0,16},{16,32},{32,48},{48,0},{1,17},{17,33},{33,49},{49,1},{2,18}... | collective-permute-start | bytes 608264 | tf_op jit(solution)/shard_map/ppermute | solution.py:27
  199.7 10.2 %collective-permute-start.42 = (bf16[24,4224]{1,0:T(8,128)(2,1)S(1)}, bf16[24,4224]{1,0:T(8,128)(2,1)S(1)}, u32[]{:S(2)}, u32[]{:S(2)}) collective-permute-start(bf16[24,4224]{1,0:T(8,128)(2,1)S(1)} %get-tuple-element.108), channel_id=1, source_target_pairs={{0,32},{16,48},{32,0},{48,16},{1,33},{17,49},{33,1},{49,17},{2,34}... | collective-permute-start | bytes 608264 | tf_op jit(solution)/shard_map/ppermute | solution.py:27
  (33 other events, 234.1 us)
where the time goes:
time: 226 us; the launch traced here: 222 us
  starting transfers between devices  86.2 us (38%)
  Pallas kernels  58.5 us (26%)
  waiting for transfers between devices  58 us (26%)
  other arithmetic  11.4 us (5%)
  local copies, waits for them, and re-layouts  6.87 us (3%)
    pallas_call x5, Pallas kernels, call(): pl.pallas_call(kernel, out_shape=shapes, in_specs=[pl.BlockSpec(memory_sp...  50.7 us
    ppermute x18, waiting for transfers between devices, line_send(): return lax.ppermute(value, axis, [(i, (i + step) % 4) for i in range(4)])  45.6 us
    ppermute x13, starting transfers between devices, swap_cores(): return lax.ppermute(value, 'core', [(0, 1), (1, 0)])  30.1 us
    ppermute x18, starting transfers between devices, line_send(): return lax.ppermute(value, axis, [(i, (i + step) % 4) for i in range(4)])  26.8 us
    ppermute x12, starting transfers between devices, line_send(): return lax.ppermute(value, X, [(i, i ^ step) for i in range(4)])  21.7 us
    convert_element_type x5, other arithmetic, chooser(): (jnp.arange(count, dtype=jnp.int32)[:, None] == natural[None, :]).astype(...  8.83 us
    ppermute x12, waiting for transfers between devices, line_send(): return lax.ppermute(value, X, [(i, i ^ step) for i in range(4)])  7.96 us
  transfers between devices with their start and end apart: 47, of which 20 were waited for; matrix products, arithmetic and copies ran while one was open for 6% of the time, Pallas kernels for 15%

commit v1 on v0

--- a/solution.py
+++ b/solution.py
@@ -43,12 +43,11 @@
 def owner_rows(first):
     index = jnp.arange(768, dtype=jnp.int32)
     core = (index // 384) ^ lax.axis_index("core")
-    step, turn = (index // 96) % 4, (index // 24) % 4
-    if first == "y":
-        step, turn = turn, step
+    one, two, three = (index // 96) % 4, (index // 24) % 4, (index // 6) % 4
+    step, up, turn = (one, two, three) if first == "x" else (two, three, one)
     line = (lax.axis_index("x_lo") * 2 + lax.axis_index("x_hi")) ^ step
     y = (lax.axis_index("y") - turn) % 4
-    z = (lax.axis_index("z") - (index // 6) % 4) % 4
+    z = (lax.axis_index("z") - up) % 4
     device = (((line // 2) * 4 + y) * 4 + z) * 4 + (line % 2) * 2 + core
     return device * 6 + index % 6
 
@@ -59,12 +58,7 @@
 
 def down_choosers(natural):
     device, row = natural // 6, natural % 6
-    late = device * 9 + 6 + row // 2
-    return (
-        chooser(device * 9 + row, 1152),
-        chooser(jnp.where(row % 2 == 0, late, -1), 1152),
-        chooser(jnp.where(row % 2 == 1, late, -1), 1152),
-    )
+    return chooser(device * 9 + row, 1152), chooser(device * 9 + 6 + row // 2, 1152)
 
 
 def dot(a, b):
@@ -121,10 +115,11 @@
 def project_kernel(*refs):
     pieces = refs[:8]
     tokens, choose, cosine, sine, marks = refs[8:13]
-    queries, key_values, ordered, gains, weight, sems = refs[13:]
+    queries, key_values, ordered, gains, kept, weight, sems, out_sems = refs[13:]
     copies = load_pieces(pieces, weight, sems, 0)
     unit, _ = normed(tokens[...].astype(F32))
     wait_all(copies)
+    sent = send_out(weight, kept, out_sems.at[0])
     gain_order = dot_nt(unit_rows(), weight[:, 2304:]).astype(BF16)
     gain = dot_nt(gain_order, choose[...])
     gains[...] = gain
@@ -133,12 +128,13 @@
     ordered[...] = h_ord
     cos_w, sin_w = wide(cosine[...], 6), wide(sine[...], 6)
     part = dot(h_ord, weight[:, :768])
-    queries[...] = rotate(part, cos_w, sin_w).astype(BF16)
+    queries[...] = (rotate(part, cos_w, sin_w) * 0.125).astype(BF16)
     part = dot(h_ord, weight[:, 768:1536])
     key_values[:, :768] = rotate(part, cos_w, sin_w).astype(BF16)
     part = dot(h_ord, weight[:, 1536:2304])
     key_values[:, 768:1536] = part.astype(BF16)
     key_values[:, 1536:] = marks[...]
+    sent.wait()
 
 
 def load_pieces(pieces, target, sems, first):
@@ -154,6 +150,12 @@
     return copies
 
 
+def send_out(source, target, sem):
+    copy = pltpu.make_async_copy(source, target, sem)
+    copy.start()
+    return copy
+
+
 def wait_all(copies):
     for copy in copies:
         copy.wait()
@@ -191,15 +193,15 @@
 
 
 def probabilities(query_stack, keys, bias):
-    scores = dot_nt(query_stack, keys) * 0.125 + bias
+    scores = dot_nt(query_stack, keys) + bias
     expo = jnp.exp(scores - jnp.max(scores, -1, keepdims=True))
-    return expo / jnp.sum(expo, -1, keepdims=True)
+    return expo * (1.0 / jnp.sum(expo, -1, keepdims=True))
 
 
 def attend_kernel(*refs):
     pieces = refs[:8]
     queries, key_values, prev, follow, tokens, choose = refs[8:14]
-    ordered, after, span, context, weight, sems = refs[14:]
+    ordered, after, kept, span, context, weight, sems = refs[14:]
     copies = load_pieces(pieces, weight, sems, 2304)
     fill_span(span, prev, key_values, follow)
     for block in range(2):
@@ -210,7 +212,9 @@
             lanes = slice(pair * 128, pair * 128 + 128)
             value_lanes = slice(768 + pair * 128, 768 + pair * 128 + 128)
             probs = probabilities(head_stack(queries[rows, lanes]), span[cols, lanes], bias)
-            mixed = dot(probs.astype(BF16), span[cols, value_lanes])
+            low = probs.astype(BF16)
+            kept[block * 6 + pair] = low
+            mixed = dot(low, span[cols, value_lanes])
             context[rows, lanes] = head_merge(mixed).astype(BF16)
     ordered[...] = dot(context[...], choose[...]).astype(BF16)
     wait_all(copies)
@@ -219,47 +223,70 @@
 
 def feed_kernel(*refs):
     pieces = refs[:8]
-    after, gains, cotangent, context, choose_in, choose_one, choose_two, choose_three = refs[8:16]
-    mixed, grad_own, grad_other, grad_after, gain_grad, weight, d_ref, sems = refs[16:]
-    copies = load_pieces(pieces, weight, sems, 0)
+    after, gains, cotangent, context, choose_in, choose_one, choose_two = refs[8:15]
+    mixed, grad_own, grad_other, grad_after, gain_grad = refs[15:20]
+    weight, w_down, wide_ref, d_ref, hid, own_buf, other_buf = refs[20:27]
+    in_sems, down_sems, out_sems = refs[27:]
+    copies = load_pieces(pieces, weight, in_sems, 0)
+    down_copies = load_pieces(pieces, w_down, down_sems, 3072)
+    sent = []
+
+    def send_grads(first, count):
+        cols = pl.ds(first, count)
+        for buffer, target in ((other_buf, grad_other), (own_buf, grad_own)):
+            sem = out_sems.at[len(sent)]
+            sent.append(send_out(buffer.at[:, cols], target.at[:, cols], sem))
+
     x_two = after[...]
     unit, scale = normed(x_two)
     gain = gains[1:2]
     h_two = (unit * gain).astype(BF16)
     h_ord = dot(h_two, choose_in[...]).astype(BF16)
     wait_all(copies)
-    gate = dot(h_ord, weight[:, :1152])
-    up = dot(h_ord, weight[:, 1152:2304])
-    phi = 0.5 + 0.5 * lax.erf(gate * (2.0**-0.5))
-    slope = phi + gate * jnp.exp(-0.5 * gate * gate) * ((2.0 * math.pi) ** -0.5)
-    gated = gate * phi
-    hidden = (gated * up).astype(BF16)
-    hid_one = dot(hidden, choose_one[...]).astype(BF16)
-    hid_two = dot(hidden, choose_two[...]).astype(BF16)
-    hid_three = dot(hidden, choose_three[...]).astype(BF16)
-    main = dot(hid_one, weight[:, 3072:3840])
-    mixed[:, :384] = (x_two[:, :384] + main[:, :384] + dot(hid_two, weight[:, 3840:])).astype(BF16)
-    mixed[:, 384:] = (x_two[:, 384:] + main[:, 384:] + dot(hid_three, weight[:, 3840:])).astype(
+    wide_ref[...] = dot(h_ord, weight[...])
+
+    def activate(index, carry):
+        rows = pl.ds(pl.multiple_of(index * 16, 16), 16)
+        gate, up = wide_ref[rows, :1152], wide_ref[rows, 1152:]
+        phi = 0.5 + 0.5 * lax.erf(gate * (2.0**-0.5))
+        slope = phi + gate * jnp.exp(-0.5 * gate * gate) * ((2.0 * math.pi) ** -0.5)
+        gated = gate * phi
+        hid[rows, :] = (gated * up).astype(BF16)
+        wide_ref[rows, :1152] = up * slope
+        wide_ref[rows, 1152:] = gated
+        return carry
+
+    lax.fori_loop(0, 16, activate, 0)
+    hid_one = dot(hid[...], choose_one[...]).astype(BF16)
+    late = dot(hid[...], choose_two[...]).astype(BF16)
+    even = lax.broadcasted_iota(jnp.int32, (256, 768), 1) % 2 == 0
+    zero = jnp.zeros_like(late)
+    hid_two, hid_three = jnp.where(even, late, zero), jnp.where(even, zero, late)
+    wait_all(down_copies)
+    main = dot(hid_one, w_down[:, :768])
+    mixed[:, :384] = (x_two[:, :384] + main[:, :384] + dot(hid_two, w_down[:, 768:])).astype(BF16)
+    mixed[:, 384:] = (x_two[:, 384:] + main[:, 384:] + dot(hid_three, w_down[:, 768:])).astype(
         BF16
     )
     dy = cotangent[...]
     first, second = dy[:, :384], dy[:, 384:]
-    halves = ((grad_own, slice(0, 384)), (grad_other, slice(384, 768)))
+    halves = ((own_buf, slice(0, 384)), (other_buf, slice(384, 768)))
     for target, part in halves:
         target[:, 3072:3840] = dot_tn(hid_one[:, part], dy).astype(BF16)
         target[:, 3840:] = (
             dot_tn(hid_two[:, part], first) + dot_tn(hid_three[:, part], second)
         ).astype(BF16)
-    d_hidden = (
-        dot_nt(dot_nt(dy, weight[:, 3072:3840]).astype(BF16), choose_one[...])
-        + dot_nt(dot_nt(first, weight[:, 3840:]).astype(BF16), choose_two[...])
-        + dot_nt(dot_nt(second, weight[:, 3840:]).astype(BF16), choose_three[...])
-    )
-    d_ref[:, :1152] = (d_hidden * up * slope).astype(BF16)
-    d_ref[:, 1152:] = (d_hidden * gated).astype(BF16)
+    send_grads(3072, 1152)
+    d_late = jnp.where(even, dot_nt(first, w_down[:, 768:]), dot_nt(second, w_down[:, 768:]))
+    d_hidden = dot_nt(dot_nt(dy, w_down[:, :768]).astype(BF16), choose_one[...]) + dot_nt(
+        d_late.astype(BF16), choose_two[...]
+    )
+    d_ref[:, :1152] = (d_hidden * wide_ref[:, :1152]).astype(BF16)
+    d_ref[:, 1152:] = (d_hidden * wide_ref[:, 1152:]).astype(BF16)
     for target, part in halves:
         target[:, :2304] = dot_tn(h_ord[:, part], d_ref[...]).astype(BF16)
-    d_ord = dot_nt(d_ref[...], weight[:, :2304])
+    send_grads(0, 2304)
+    d_ord = dot_nt(d_ref[...], weight[...])
     d_h = dot_nt(d_ord.astype(BF16), choose_in[...])
     gain_grad[...] = jnp.broadcast_to(jnp.sum(d_h * unit, 0, keepdims=True), (8, 768))
     d_after = dy.astype(F32) + norm_back(d_h, gain, unit, scale)
@@ -267,12 +294,14 @@
     low = d_after.astype(BF16)
     for target, part in halves:
         target[:, 2304:3072] = dot_tn(context[:, part], low).astype(BF16)
+    send_grads(2304, 768)
+    wait_all(sent)
 
 
 def attend_back_kernel(*refs):
     pieces = refs[:8]
-    queries, key_values, prev, follow, grad_after, choose, cosine, sine = refs[8:16]
-    grad_queries, grad_own, to_prev, to_follow, span, grads, d_ctx, weight, sems = refs[16:]
+    queries, key_values, prev, follow, grad_after, choose, cosine, sine, kept = refs[8:17]
+    grad_queries, grad_own, to_prev, to_follow, span, grads, d_ctx, weight, sems = refs[17:]
     copies = load_pieces(pieces, weight, sems, 2304)
     fill_span(span, prev, key_values, follow)
     low = grad_after[...].astype(BF16)
@@ -282,7 +311,6 @@
     grads[...] = jnp.zeros_like(grads)
     cos_n, sin_n = cosine[...], sine[...]
     for block in range(2):
-        bias = visible(span, block)
         rows = slice(block * 128, block * 128 + 128)
         cols = slice(block * 128, block * 128 + 256)
         for pair in range(6):
@@ -290,7 +318,8 @@
             value_lanes = slice(768 + pair * 128, 768 + pair * 128 + 128)
             query_stack = head_stack(queries[rows, lanes])
             keys = span[cols, lanes]
-            probs = probabilities(query_stack, keys, bias)
+            low_probs = kept[block * 6 + pair]
+            probs = low_probs.astype(F32)
             d_stack = head_stack(d_ctx[rows, lanes])
             d_probs = dot_nt(d_stack, span[cols, value_lanes])
             delta = jnp.sum(d_probs * probs, -1, keepdims=True)
@@ -299,15 +328,14 @@
             grad_queries[rows, lanes] = rotate_back(
                 d_query, cos_n[rows], sin_n[rows]
             ).astype(BF16)
-            grads[cols, lanes] += dot_tn(d_scores, query_stack) * 0.125
-            grads[cols, value_lanes] += dot_tn(probs.astype(BF16), d_stack)
+            grads[cols, lanes] += dot_tn(d_scores, query_stack)
+            grads[cols, value_lanes] += dot_tn(low_probs, d_stack)
     to_prev[...] = grads[:64].astype(BF16)
     to_follow[...] = grads[320:].astype(BF16)
     grad_own[...] = grads[64:320]
 
 
 def project_back_kernel(*refs):
-    pieces = refs[:8]
     (
         grad_queries,
         grad_own,
@@ -321,10 +349,10 @@
         sine,
         grad_after,
         gain_two_grad,
-    ) = refs[8:20]
-    input_grad, weight_own, *weight_other = refs[20:26]
-    grad_kv, d_qkv, weight, sems = refs[26:]
-    copies = load_pieces(pieces, weight, sems, 0)
+        weight,
+    ) = refs[:13]
+    input_grad, weight_own, *weight_other = refs[13:19]
+    grad_kv, d_qkv, own_buf, other_buf, out_sems = refs[19:]
     grad_kv[...] = grad_own[...]
     grad_kv[:64] += from_prev[...].astype(F32)
     grad_kv[192:] += from_follow[...].astype(F32)
@@ -334,11 +362,19 @@
     d_qkv[:, 1536:] = grad_kv[:, 768:].astype(BF16)
     grad = d_qkv[...]
     h_ord = ordered[...]
-    weight_own[:, :2304] = dot_tn(h_ord[:, :384], grad).astype(BF16)
-    far_grad = dot_tn(h_ord[:, 384:], grad).astype(BF16)
-    for quarter, part in enumerate(weight_other):
-        part[:, :2304] = far_grad[96 * quarter : 96 * quarter + 96]
-    wait_all(copies)
+    sent = []
+
+    def send_grads(cols):
+        for quarter, part in enumerate(weight_other):
+            rows = pl.ds(96 * quarter, 96)
+            sem = out_sems.at[len(sent)]
+            sent.append(send_out(other_buf.at[rows, cols], part.at[:, cols], sem))
+        sem = out_sems.at[len(sent)]
+        sent.append(send_out(own_buf.at[:, cols], weight_own.at[:, cols], sem))
+
+    other_buf[:, :2304] = dot_tn(h_ord[:, 384:], grad).astype(BF16)
+    own_buf[:, :2304] = dot_tn(h_ord[:, :384], grad).astype(BF16)
+    send_grads(pl.ds(0, 2304))
     d_ord = dot_nt(grad, weight[:, :2304]).astype(BF16)
     d_h = dot_nt(d_ord, choose[...])
     unit, scale = normed(tokens[...].astype(F32))
@@ -348,23 +384,25 @@
     both = jnp.where(row == 0, first, jnp.where(row == 1, gain_two_grad[0:1], 0.0))
     gain_order = dot(both.astype(BF16), choose[...]).astype(BF16)
     picks = unit_rows()
-    weight_own[:, 2304:] = dot_tn(gain_order[:, :384], picks).astype(BF16)
-    gain_cols = dot_tn(gain_order[:, 384:], picks).astype(BF16)
-    for quarter, part in enumerate(weight_other):
-        part[:, 2304:] = gain_cols[96 * quarter : 96 * quarter + 96]
-
-
-def call(kernel, outs, pieces, args, flops, scratch):
-    shapes = [jax.ShapeDtypeStruct(shape, dtype) for shape, dtype in outs]
+    own_buf[:, 2304:] = dot_tn(gain_order[:, :384], picks).astype(BF16)
+    other_buf[:, 2304:] = dot_tn(gain_order[:, 384:], picks).astype(BF16)
+    send_grads(pl.ds(2304, 128))
+    wait_all(sent)
+
+
+def call(kernel, outs, pieces, args, flops, scratch, out_copies=0):
+    shapes = [jax.ShapeDtypeStruct(tuple(shape), dtype) for shape, dtype in outs]
+    far = pl.BlockSpec(memory_space=pl.ANY)
     size = sum(v.size * v.dtype.itemsize for v in list(pieces) + list(args) + shapes)
     whole = pl.BlockSpec(memory_space=pltpu.VMEM)
     return pl.pallas_call(
         kernel,
         out_shape=shapes,
         in_specs=[pl.BlockSpec(memory_space=pl.ANY)] * len(pieces) + [whole] * len(args),
-        out_specs=[whole] * len(outs),
+        out_specs=[far if isinstance(shape, list) else whole for shape, _ in outs],
         scratch_shapes=[pltpu.VMEM(shape, dtype) for shape, dtype in scratch]
-        + [pltpu.SemaphoreType.DMA((8,))] * ((len(pieces) + 7) // 8),
+        + [pltpu.SemaphoreType.DMA((max(len(pieces), 1),))] * (2 if out_copies == 6 else len(pieces) // 8)
+        + [pltpu.SemaphoreType.DMA((out_copies,))] * (out_copies > 0),
         compiler_params=pltpu.CompilerParams(vmem_limit_bytes=48 * 1024 * 1024),
         cost_estimate=pl.CostEstimate(
             flops=int(flops), bytes_accessed=size if flops > 1 else 1, transcendentals=0
@@ -386,7 +424,7 @@
     )(*args)
 
 
-def pack_kernel(qkv, out, gate_up, down, gain_one, gain_two, packed):
+def pack_kernel(qkv, out, gate_up, down, gain_one, gain_two, packed, rest):
     row = lax.broadcasted_iota(jnp.int32, (6, 6), 0)
     col = lax.broadcasted_iota(jnp.int32, (6, 6), 1)
     one = jnp.sum(jnp.where(row == col, gain_one[...].astype(F32), 0.0), 1, keepdims=True)
@@ -395,18 +433,19 @@
     gains = jnp.where(lane == 0, one, jnp.where(lane == 1, two, 0.0))
     packed[:, :2304] = qkv[...]
     packed[:, 2304:2432] = gains.astype(BF16)
-    packed[:, 2432:4736] = gate_up[...]
-    packed[:, 4736:5504] = out[...]
+    rest[:, :2304] = gate_up[...]
+    rest[:, 2304:3072] = out[...]
     rows = down[...].astype(F32)
-    packed[:, 5504:6272] = rows[:6].astype(BF16)
+    rest[:, 3072:3840] = rows[:6].astype(BF16)
     halves = []
     for index in range(6, 9):
         halves += [rows[index : index + 1, :384], rows[index : index + 1, 384:]]
-    packed[:, 6272:] = jnp.concatenate(halves, 0).astype(BF16)
+    rest[:, 3840:] = jnp.concatenate(halves, 0).astype(BF16)
 
 
 def stack_kernel(*refs):
-    refs[-1][...] = jnp.concatenate([ref[...].astype(F32) for ref in refs[:-1]], 0).astype(BF16)
+    both = jnp.concatenate([ref[...].astype(F32) for ref in refs[:-1]], 0).astype(BF16)
+    refs[-1][...] = both
 
 
 def fold_kernel(own, *refs):
@@ -466,9 +505,9 @@
     down_weight,
     cotangent,
 ):
-    shard = small_call(
+    shard_a, shard_b = small_call(
         pack_kernel,
-        jax.ShapeDtypeStruct((6, 6656), BF16),
+        [jax.ShapeDtypeStruct((6, 2432), BF16), jax.ShapeDtypeStruct((6, 4224), BF16)],
         (
             qkv_weight,
             out_weight,
@@ -478,12 +517,11 @@
             norm_two.reshape(1, 6),
         ),
     )
-    slabs = line_gather(shard, "z")
-    block_a = jnp.concatenate([v[:, :2432] for v in slabs], 0)
-    block_b = jnp.concatenate([v[:, 2432:] for v in slabs], 0)
-    block_a = jnp.concatenate(line_gather(block_a, "x"), 0)
-    lines_b = line_gather(block_b, "y")
-    block_a = after_these(block_a, lines_b)
+    lines_a = line_gather(shard_a, "z")
+    lines_b = line_gather(shard_b, "y")
+    block_a, block_b = jnp.concatenate(lines_a, 0), jnp.concatenate(lines_b, 0)
+    lines_a, lines_b = line_gather(block_a, "x"), line_gather(block_b, "z")
+    block_a = jnp.concatenate(lines_a, 0)
     block_b = small_call(stack_kernel, jax.ShapeDtypeStruct((96, 4224), BF16), lines_b)
     lines_a = [block_a] + [line_send(block_a, "y", step) for step in (1, 2, 3)]
     pieces_a = lines_a + [swap_cores(v) for v in lines_a]
@@ -499,9 +537,15 @@
     place = (lax.axis_index("z") * 2 + lax.axis_index("x_hi")) * 2 + lax.axis_index("core")
     cosine, sine = angle_tables(place * 256)
 
-    queries, key_values, ordered, gain_rows = call(
+    queries, key_values, ordered, gain_rows, w_qkv = call(
         project_kernel,
-        [((256, 768), BF16), ((256, 1664), BF16), ((256, 768), BF16), ((8, 768), F32)],
+        [
+            ((256, 768), BF16),
+            ((256, 1664), BF16),
+            ((256, 768), BF16),
+            ((8, 768), F32),
+            ([768, 2432], BF16),
+        ],
         pieces_a,
         (
             after_these(inputs, choose_b, choose_d, near_b),
@@ -512,6 +556,7 @@
         ),
         4e9,
         [((768, 2432), BF16)],
+        1,
     )
     prev = lax.ppermute(key_values[192:], SEQ, next_pairs(1))
     follow = lax.ppermute(key_values[:64], SEQ, next_pairs(-1))
@@ -519,9 +564,9 @@
     block_b, near_b = after_these((block_b, near_b), gain_rows)
     lines_b = [block_b, far_b] + near_b
     pieces_b = lines_b + [swap_cores(v) for v in lines_b]
-    context, after = call(
+    context, after, probs = call(
         attend_kernel,
-        [((256, 768), BF16), ((256, 768), F32)],
+        [((256, 768), BF16), ((256, 768), F32), ((12, 256, 256), BF16)],
         pieces_b,
         (queries, key_values, prev, follow, inputs, choose_b),
         4e9,
@@ -531,21 +576,30 @@
         feed_kernel,
         [
             ((256, 768), BF16),
-            ((384, 4224), BF16),
-            ((384, 4224), BF16),
+            ([384, 4224], BF16),
+            ([384, 4224], BF16),
             ((256, 768), F32),
             ((8, 768), F32),
         ],
         pieces_b,
         (after, gain_rows, cotangent[0], context, choose_b) + choose_d,
         15e9,
-        [((768, 4224), BF16), ((256, 2304), BF16)],
+        [
+            ((768, 2304), BF16),
+            ((768, 1152), BF16),
+            ((256, 2304), F32),
+            ((256, 2304), BF16),
+            ((256, 1152), BF16),
+            ((384, 4224), BF16),
+            ((384, 4224), BF16),
+        ],
+        6,
     )
     grad_queries, grad_kv, to_prev, to_follow = call(
         attend_back_kernel,
         [((256, 768), BF16), ((256, 1536), F32), ((64, 1536), BF16), ((64, 1536), BF16)],
         pieces_b,
-        (queries, key_values, prev, follow, grad_after, choose_b, cosine, sine),
+        (queries, key_values, prev, follow, grad_after, choose_b, cosine, sine, probs),
         10e9,
         [
             ((384, 1664), BF16),
@@ -563,8 +617,8 @@
     rest_far = line_send(after_these(rest_parts[0], rest_near), "x", 1)
     input_grad, qkv_own, *qkv_other = call(
         project_back_kernel,
-        [((256, 768), BF16), ((384, 2432), BF16)] + [((96, 2432), BF16)] * 4,
-        pieces_a,
+        [((256, 768), BF16), ([384, 2432], BF16)] + [([96, 2432], BF16)] * 4,
+        [],
         (
             after_these(grad_queries, rest_parts),
             grad_kv,
@@ -578,17 +632,25 @@
             sine,
             grad_after,
             gain_two_grad,
+            w_qkv,
         ),
         1,
-        [((256, 1536), F32), ((256, 2304), BF16), ((768, 2432), BF16)],
+        [
+            ((256, 1536), F32),
+            ((256, 2304), BF16),
+            ((384, 2432), BF16),
+            ((384, 2432), BF16),
+        ],
+        10,
     )
     qkv_own = after_these(qkv_own, rest_near)
     qkv_mine, *qkv_parts = fold(qkv_own, [swap_cores(v) for v in qkv_other])
     qkv_lines = [line_send(part, "y", 4 - step) for step, part in zip((1, 2, 3), qkv_parts)]
+    rest_total = line_total(rest_mine, rest_near + [rest_far])
     half_a = line_sum(line_total(qkv_mine, qkv_lines), "x")
-    half_b = line_sum(line_total(rest_mine, rest_near + [rest_far]), "y")
-    owned = line_sum(jnp.concatenate([half_a, half_b], 1), "z")
-    owned_a, owned_b = owned[:, :2432], owned[:, 2432:]
+    half_b = line_sum(rest_total, "z")
+    half_a, half_b = lax.optimization_barrier((half_a, half_b))
+    owned_a, owned_b = line_sum(half_a, "z"), line_sum(half_b, "y")
     owned_down = jnp.concatenate([owned_b[:, 3072:3840], owned_b[:, 3840:].reshape(3, 768)], 0)
     return (
         mixed[None],

time: 226 us -> 225 us (level)
  starting transfers between devices: 86.2 us -> 92.7 us
  waiting for transfers between devices: 58 us -> 52 us
  Pallas kernels: 58.5 us -> 54.4 us
    ppermute x18 -> x24, waiting for transfers between devices: 45.6 us -> 36.3 us  [line_send(): return lax.ppermute(value, axis, [(i, (i + step) % 4) for i in range(4)])]
    ppermute x18 -> x24, starting transfers between devices: 26.8 us -> 35.5 us  [line_send(): return lax.ppermute(value, axis, [(i, (i + step) % 4) for i in range(4)])]
    ppermute x12, waiting for transfers between devices: 7.96 us -> 12.6 us  [line_send(): return lax.ppermute(value, X, [(i, i ^ step) for i in range(4)])]
    pallas_call x5, Pallas kernels: 50.7 us -> 46.7 us  [call(): pl.pallas_call(kernel, out_shape=shapes, in_specs=[pl.BlockSpec(memory_sp...]
    ppermute x13, starting transfers between devices: 30.1 us -> 26.6 us  [swap_cores(): return lax.ppermute(value, 'core', [(0, 1), (1, 0)])]
    unnamed x36 -> x30, local copies, waits for them, and re-layouts: 2.45 us -> 4.89 us
    convert_element_type x5 -> x4, other arithmetic: 8.83 us -> 6.87 us  [chooser(): (jnp.arange(count, dtype=jnp.int32)[:, None] == natural[None, :]).astype(...]
  transfers between devices with their start and end apart: 47 -> 53, of which waited for: 20 -> 20; matrix products, arithmetic and copies ran while one was open for 6% -> 6% of each run, Pallas kernels for 15% -> 14%
where the time goes in v1:
time: 225 us; the launch traced here: 221 us
  starting transfers between devices  92.7 us (41%)
  Pallas kernels  54.4 us (24%)
  waiting for transfers between devices  52 us (23%)
  other arithmetic  11.7 us (5%)
  local copies, waits for them, and re-layouts  8.98 us (4%)
    pallas_call x5, Pallas kernels, call(): pl.pallas_call(kernel, out_shape=shapes, in_specs=[pl.BlockSpec(memory_sp...  46.7 us
    ppermute x24, waiting for transfers between devices, line_send(): return lax.ppermute(value, axis, [(i, (i + step) % 4) for i in range(4)])  36.3 us
    ppermute x24, starting transfers between devices, line_send(): return lax.ppermute(value, axis, [(i, (i + step) % 4) for i in range(4)])  35.5 us
    ppermute x13, starting transfers between devices, swap_cores(): return lax.ppermute(value, 'core', [(0, 1), (1, 0)])  26.6 us
    ppermute x12, starting transfers between devices, line_send(): return lax.ppermute(value, X, [(i, i ^ step) for i in range(4)])  23 us
    ppermute x12, waiting for transfers between devices, line_send(): return lax.ppermute(value, X, [(i, i ^ step) for i in range(4)])  12.6 us
    convert_element_type x4, other arithmetic, chooser(): (jnp.arange(count, dtype=jnp.int32)[:, None] == natural[None, :]).astype(...  6.87 us
    unnamed x30, local copies, waits for them, and re-layouts  4.89 us
  transfers between devices with their start and end apart: 53, of which 20 were waited for; matrix products, arithmetic and copies ran while one was open for 6% of the time, Pallas kernels for 14%

profile of v1, /device:TPU:2, one launch (start us, length us, event | category | flops | bytes accessed | tf_op | source)
XLA Modules:
  0.0 221.1 jit_solution(16709577124845052096)
XLA Ops:
  2.2 4.0 %collective-permute-start.10 = (bf16[6,2432]{1,0:T(8,128)(2,1)}, bf16[6,2432]{1,0:T(8,128)(2,1)S(1)}, u32[]{:S(2)}, u32[]{:S(2)}) collective-permute-start(bf16[6,2432]{1,0:T(8,128)(2,1)} %get-tuple-element.59), channel_id=1, source_target_pairs={{0,12},{4,0},{8,4},{12,8},{1,13},{5,1},{9,5},{13,9},{2,14},{6,2},{... | collective-permute-start | bytes 87560 | tf_op jit(solution)/shard_map/ppermute | solution.py:27
  7.5 3.0 %collective-permute-start.2 = (bf16[6,4224]{1,0:T(8,128)(2,1)}, bf16[6,4224]{1,0:T(8,128)(2,1)S(1)}, u32[]{:S(2)}, u32[]{:S(2)}) collective-permute-start(bf16[6,4224]{1,0:T(8,128)(2,1)} %get-tuple-element.58), channel_id=1, source_target_pairs={{0,48},{16,0},{32,16},{48,32},{1,49},{17,1},{33,17},{49,33},{2,50}... | collective-permute-start | bytes 152072 | tf_op jit(solution)/shard_map/ppermute | solution.py:27
  19.5 2.0 collective-permute-start.5
  21.5 2.3 %collective-permute-start.4 = (bf16[24,4224]{1,0:T(8,128)(2,1)S(1)}, bf16[24,4224]{1,0:T(8,128)(2,1)S(1)}, u32[]{:S(2)}, u32[]{:S(2)}) collective-permute-start(bf16[24,4224]{1,0:T(8,128)(2,1)S(1)} %pad_maximum_fusion.refs_0_), channel_id=1, source_target_pairs={{0,8},{4,12},{8,0},{12,4},{1,9},{5,13},{9,1},{13,5},{2,10},{6,14},... | collective-permute-start | bytes 608264 | tf_op jit(solution)/shard_map/ppermute | solution.py:27
  25.5 2.3 %collective-permute-start.16 = (bf16[96,2432]{1,0:T(8,128)(2,1)S(1)}, bf16[96,2432]{1,0:T(8,128)(2,1)S(1)}, u32[]{:S(2)}, u32[]{:S(2)}) collective-permute-start(bf16[96,2432]{1,0:T(8,128)(2,1)S(1)} %concatenate.21.refs_0_), channel_id=1, source_target_pairs={{0,48},{16,0},{32,16},{48,32},{1,49},{17,1},{33,17},{49,33},{2,50}... | collective-permute-start | bytes 1400840 | tf_op jit(solution)/shard_map/ppermute | solution.py:27
  30.2 2.1 collective-permute-done.3.refs_1_
  33.0 2.2 stack_kernel.1.refs_0_
  46.1 3.2 %collective-permute-done.14.refs_1_ = bf16[96,2432]{1,0:T(8,128)(2,1)S(1)} collective-permute-done((bf16[96,2432]{1,0:T(8,128)(2,1)S(1)}, bf16[96,2432]{1,0:T(8,128)(2,1)S(1)}, u32[]{:S(2)}, u32[]{:S(2)}) %collective-permute-start.14) | collective-permute-done | bytes 466976 | tf_op jit(solution)/shard_map/ppermute | solution.py:27
  49.3 4.2 %collective-permute-done.7.refs_3_ = bf16[96,4224]{1,0:T(8,128)(2,1)S(1)} collective-permute-done((bf16[96,4224]{1,0:T(8,128)(2,1)}, bf16[96,4224]{1,0:T(8,128)(2,1)S(1)}, u32[]{:S(2)}, u32[]{:S(2)}) %collective-permute-start.7) | collective-permute-done | bytes 811040 | tf_op jit(solution)/shard_map/ppermute | solution.py:26
  57.6 6.4 %project_kernel.1 = (bf16[256,768]{1,0:T(8,128)(2,1)S(1)}, bf16[256,1664]{1,0:T(8,128)(2,1)S(1)}, bf16[256,768]{1,0:T(8,128)(2,1)S(1)}, f32[8,768]{1,0:T(8,128)S(1)}, bf16[768,2432]{1,0:T(8,128)(2,1)}) custom-call(bf16[96,2432]{1,0:T(8,128)(2,1)S(1)} %concatenate.21.refs_0_, bf16[96,2432]{1,0:T(8,128)(2,1)S(1)} %collective-permute-done.14.refs_1_, ...), custom_call_target="tpu_custom_call" | custom-call | flops 4000000000 | bytes 11034624 | tf_op jit(solution)/shard_map/project_kernel/pallas_call | solution.py:398
  65.4 3.0 %collective-permute-start.22 = (bf16[64,1664]{1,0:T(8,128)(2,1)S(1)}, bf16[64,1664]{1,0:T(8,128)(2,1)S(1)}, u32[]{:S(2)}, u32[]{:S(2)}) collective-permute-start(bf16[64,1664]{1,0:T(8,128)(2,1)S(1)} %get-tuple-element.115), channel_id=1, source_target_pairs={{0,1},{1,2},{2,3},{3,4},{4,5},{5,6},{6,7},{7,8},{8,9},{9,10},{10,1... | collective-permute-start | bytes 638984 | tf_op jit(solution)/shard_map/ppermute | solution.py:561
  68.4 3.0 %collective-permute-start.24 = (bf16[96,4224]{1,0:T(8,128)(2,1)S(1)}, bf16[96,4224]{1,0:T(8,128)(2,1)S(1)}, u32[]{:S(2)}, u32[]{:S(2)}) collective-permute-start(bf16[96,4224]{1,0:T(8,128)(2,1)S(1)} %copy-done.2), channel_id=1, source_target_pairs={{0,1},{1,0},{2,3},{3,2},{4,5},{5,4},{6,7},{7,6},{8,9},{9,8},{10,11... | collective-permute-start | bytes 2433032 | tf_op jit(solution)/shard_map/ppermute | solution.py:21
  71.5 10.5 %collective-permute-start.27 = (bf16[96,4224]{1,0:T(8,128)(2,1)S(1)}, bf16[96,4224]{1,0:T(8,128)(2,1)S(1)}, u32[]{:S(2)}, u32[]{:S(2)}) collective-permute-start(bf16[96,4224]{1,0:T(8,128)(2,1)S(1)} %collective-permute-done.7.refs_3_), channel_id=1, source_target_pairs={{0,1},{1,0},{2,3},{3,2},{4,5},{5,4},{6,7},{7,6},{8,9},{9,8},{10,11... | collective-permute-start | bytes 2433032 | tf_op jit(solution)/shard_map/ppermute | solution.py:21
  86.1 5.4 %attend_kernel.1 = (bf16[256,768]{1,0:T(8,128)(2,1)S(1)}, f32[256,768]{1,0:T(8,128)S(1)}, bf16[12,256,256]{2,1,0:T(8,128)(2,1)}) custom-call(bf16[96,4224]{1,0:T(8,128)(2,1)S(1)} %copy-done.2, bf16[96,4224]{1,0:T(8,128)(2,1)S(1)} %collective-permute-done.21.refs_1_, bf16[96,4224]{1,0:T(8,128)(2,1)S(1)} %collective-permute-done.6.refs_2_, ...), custom_call_target="tpu_custom_call" | custom-call | flops 4000000000 | bytes 12484608 | tf_op jit(solution)/shard_map/attend_kernel/pallas_call | solution.py:398
  91.5 16.6 %feed_kernel.1 = (bf16[256,768]{1,0:T(8,128)(2,1)}, bf16[384,4224]{1,0:T(8,128)(2,1)}, bf16[384,4224]{1,0:T(8,128)(2,1)}, f32[256,768]{1,0:T(8,128)S(1)}, f32[8,768]{1,0:T(8,128)S(1)}) custom-call(bf16[96,4224]{1,0:T(8,128)(2,1)S(1)} %copy-done.2, bf16[96,4224]{1,0:T(8,128)(2,1)S(1)} %collective-permute-done.21.refs_1_, ...), custom_call_target="tpu_custom_call" | custom-call | flops 15000000512 | bytes 20496384 | tf_op jit(solution)/shard_map/feed_kernel/pallas_call | solution.py:398
  108.1 9.2 %collective-permute-start.28 = (bf16[384,4224]{1,0:T(8,128)(2,1)}, bf16[384,4224]{1,0:T(8,128)(2,1)S(1)}, u32[]{:S(2)}, u32[]{:S(2)}) collective-permute-start(bf16[384,4224]{1,0:T(8,128)(2,1)} %get-tuple-element.79), channel_id=1, source_target_pairs={{0,1},{1,0},{2,3},{3,2},{4,5},{5,4},{6,7},{7,6},{8,9},{9,8},{10,11... | collective-permute-start | bytes 9732104 | tf_op jit(solution)/shard_map/ppermute | solution.py:21
  117.3 10.0 %attend_back_kernel.1 = (bf16[256,768]{1,0:T(8,128)(2,1)S(1)}, f32[256,1536]{1,0:T(8,128)}, bf16[64,1536]{1,0:T(8,128)(2,1)S(1)}, bf16[64,1536]{1,0:T(8,128)(2,1)S(1)}) custom-call(bf16[96,4224]{1,0:T(8,128)(2,1)S(1)} %copy-done.2, bf16[96,4224]{1,0:T(8,128)(2,1)S(1)} %collective-permute-done.21.refs_1_, ...), custom_call_target="tpu_custom_call" | custom-call | flops 10000000000 | bytes 14319616 | tf_op jit(solution)/shard_map/attend_back_kernel/pallas_call | solution.py:398
  132.5 3.6 %fold_kernel.2 = (f32[96,4224]{1,0:T(8,128)S(1)}, bf16[96,4224]{1,0:T(8,128)(2,1)S(1)}, bf16[96,4224]{1,0:T(8,128)(2,1)S(1)}, bf16[96,4224]{1,0:T(8,128)(2,1)S(1)}) custom-call(bf16[384,4224]{1,0:T(8,128)(2,1)} %get-tuple-element.78.own, bf16[384,4224]{1,0:T(8,128)(2,1)} %copy-done.6), custom_call_target="tpu_custom_call" | custom-call | flops 1 | bytes 1 | tf_op jit(solution)/shard_map/fold_kernel/pallas_call | solution.py:463
  136.5 5.5 %collective-permute-start.32 = (bf16[96,4224]{1,0:T(8,128)(2,1)S(1)}, bf16[96,4224]{1,0:T(8,128)(2,1)S(1)}, u32[]{:S(2)}, u32[]{:S(2)}) collective-permute-start(bf16[96,4224]{1,0:T(8,128)(2,1)S(1)} %get-tuple-element.87), channel_id=1, source_target_pairs={{0,66},{2,64},{64,2},{66,0},{1,67},{3,65},{65,3},{67,1},{4,70},{6,... | collective-permute-start | bytes 2433032 | tf_op jit(solution)/shard_map/ppermute | solution.py:26
  142.1 8.3 %project_back_kernel.1 = (bf16[256,768]{1,0:T(8,128)(2,1)}, bf16[384,2432]{1,0:T(8,128)(2,1)}, bf16[96,2432]{1,0:T(8,128)(2,1)S(1)}, bf16[96,2432]{1,0:T(8,128)(...) custom-call(bf16[256,768]{1,0:T(8,128)(2,1)S(1)} %get-tuple-element.88.refs_0_, ...), custom_call_target="tpu_custom_call" | custom-call | flops 1 | bytes 1 | tf_op jit(solution)/shard_map/project_back_kernel/pallas_call | solution.py:398
  151.1 3.8 %collective-permute-done.31 = bf16[96,4224]{1,0:T(8,128)(2,1)S(1)} collective-permute-done((bf16[96,4224]{1,0:T(8,128)(2,1)S(1)}, bf16[96,4224]{1,0:T(8,128)(2,1)S(1)}, u32[]{:S(2)}, u32[]{:S(2)}) %collective-permute-start.31) | collective-permute-done | bytes 811040 | tf_op jit(solution)/shard_map/ppermute | solution.py:26
  154.9 2.4 %collective-permute-start.36 = (bf16[96,2432]{1,0:T(8,128)(2,1)S(1)}, bf16[96,2432]{1,0:T(8,128)(2,1)S(1)}, u32[]{:S(2)}, u32[]{:S(2)}) collective-permute-start(bf16[96,2432]{1,0:T(8,128)(2,1)S(1)} %get-tuple-element.99), channel_id=1, source_target_pairs={{0,1},{1,0},{2,3},{3,2},{4,5},{5,4},{6,7},{7,6},{8,9},{9,8},{10,11... | collective-permute-start | bytes 1400840 | tf_op jit(solution)/shard_map/ppermute | solution.py:21
  157.3 3.1 %collective-permute-done.32 = bf16[96,4224]{1,0:T(8,128)(2,1)S(1)} collective-permute-done((bf16[96,4224]{1,0:T(8,128)(2,1)S(1)}, bf16[96,4224]{1,0:T(8,128)(2,1)S(1)}, u32[]{:S(2)}, u32[]{:S(2)}) %collective-permute-start.32) | collective-permute-done | bytes 811040 | tf_op jit(solution)/shard_map/ppermute | solution.py:26
  166.5 3.5 %collective-permute-start.43 = (bf16[96,4224]{1,0:T(8,128)(2,1)S(1)}, bf16[96,4224]{1,0:T(8,128)(2,1)S(1)}, u32[]{:S(2)}, u32[]{:S(2)}) collective-permute-start(bf16[96,4224]{1,0:T(8,128)(2,1)S(1)} %get-tuple-element.105), channel_id=1, source_target_pairs={{0,2},{2,0},{64,66},{66,64},{1,3},{3,1},{65,67},{67,65},{4,6},{6,4... | collective-permute-start | bytes 2433032 | tf_op jit(solution)/shard_map/ppermute | solution.py:26
  169.9 6.1 %collective-permute-done.37 = bf16[96,2432]{1,0:T(8,128)(2,1)S(1)} collective-permute-done((bf16[96,2432]{1,0:T(8,128)(2,1)S(1)}, bf16[96,2432]{1,0:T(8,128)(2,1)S(1)}, u32[]{:S(2)}, u32[]{:S(2)}) %collective-permute-start.37) | collective-permute-done | bytes 466976 | tf_op jit(solution)/shard_map/ppermute | solution.py:27
  176.0 3.5 %collective-permute-done.38 = bf16[96,2432]{1,0:T(8,128)(2,1)S(1)} collective-permute-done((bf16[96,2432]{1,0:T(8,128)(2,1)S(1)}, bf16[96,2432]{1,0:T(8,128)(2,1)S(1)}, u32[]{:S(2)}, u32[]{:S(2)}) %collective-permute-start.38) | collective-permute-done | bytes 466976 | tf_op jit(solution)/shard_map/ppermute | solution.py:27
  179.5 7.9 %collective-permute-done.39 = bf16[96,2432]{1,0:T(8,128)(2,1)S(1)} collective-permute-done((bf16[96,2432]{1,0:T(8,128)(2,1)S(1)}, bf16[96,2432]{1,0:T(8,128)(2,1)S(1)}, u32[]{:S(2)}, u32[]{:S(2)}) %collective-permute-start.39) | collective-permute-done | bytes 466976 | tf_op jit(solution)/shard_map/ppermute | solution.py:27
  187.7 4.3 %collective-permute-start.40 = (bf16[24,2432]{1,0:T(8,128)(2,1)S(1)}, bf16[24,2432]{1,0:T(8,128)(2,1)S(1)}, u32[]{:S(2)}, u32[]{:S(2)}) collective-permute-start(bf16[24,2432]{1,0:T(8,128)(2,1)S(1)} %get-tuple-element.119), channel_id=1, source_target_pairs={{0,2},{2,0},{64,66},{66,64},{1,3},{3,1},{65,67},{67,65},{4,6},{6,4... | collective-permute-start | bytes 350216 | tf_op jit(solution)/shard_map/ppermute | solution.py:26
  193.6 2.0 collective-permute-start.44
  196.5 3.7 %collective-permute-start.45 = (bf16[24,4224]{1,0:T(8,128)(2,1)S(1)}, bf16[24,4224]{1,0:T(8,128)(2,1)S(1)}, u32[]{:S(2)}, u32[]{:S(2)}) collective-permute-start(bf16[24,4224]{1,0:T(8,128)(2,1)S(1)} %get-tuple-element.118), channel_id=1, source_target_pairs={{0,8},{4,12},{8,0},{12,4},{1,9},{5,13},{9,1},{13,5},{2,10},{6,14},... | collective-permute-start | bytes 608264 | tf_op jit(solution)/shard_map/ppermute | solution.py:27
  200.3 2.1 collective-permute-done.44
  203.9 4.0 %collective-permute-done.45 = bf16[24,4224]{1,0:T(8,128)(2,1)S(1)} collective-permute-done((bf16[24,4224]{1,0:T(8,128)(2,1)S(1)}, bf16[24,4224]{1,0:T(8,128)(2,1)S(1)}, u32[]{:S(2)}, u32[]{:S(2)}) %collective-permute-start.45) | collective-permute-done | bytes 202784 | tf_op jit(solution)/shard_map/ppermute | solution.py:27
  (148 shorter events, 66.3 us)
Async XLA Ops:
  2.2 10.5 %collective-permute-start.10 = (bf16[6,2432]{1,0:T(8,128)(2,1)}, bf16[6,2432]{1,0:T(8,128)(2,1)S(1)}, u32[]{:S(2)}, u32[]{:S(2)}) collective-permute-start(bf16[6,2432]{1,0:T(8,128)(2,1)} %get-tuple-element.59), channel_id=1, source_target_pairs={{0,12},{4,0},{8,4},{12,8},{1,13},{5,1},{9,5},{13,9},{2,14},{6,2},{... | collective-permute-start | bytes 87560 | tf_op jit(solution)/shard_map/ppermute | solution.py:27
  7.5 10.5 %collective-permute-start.2 = (bf16[6,4224]{1,0:T(8,128)(2,1)}, bf16[6,4224]{1,0:T(8,128)(2,1)S(1)}, u32[]{:S(2)}, u32[]{:S(2)}) collective-permute-start(bf16[6,4224]{1,0:T(8,128)(2,1)} %get-tuple-element.58), channel_id=1, source_target_pairs={{0,48},{16,0},{32,16},{48,32},{1,49},{17,1},{33,17},{49,33},{2,50}... | collective-permute-start | bytes 152072 | tf_op jit(solution)/shard_map/ppermute | solution.py:27
  14.6 9.3 %collective-permute-start.13 = (bf16[24,2432]{1,0:T(8,128)(2,1)S(1)}, bf16[24,2432]{1,0:T(8,128)(2,1)S(1)}, u32[]{:S(2)}, u32[]{:S(2)}) collective-permute-start(bf16[24,2432]{1,0:T(8,128)(2,1)S(1)} %pad_maximum_fusion.3), channel_id=1, source_target_pairs={{0,66},{2,64},{64,2},{66,0},{1,67},{3,65},{65,3},{67,1},{4,70},{6,... | collective-permute-start | bytes 350216 | tf_op jit(solution)/shard_map/ppermute | solution.py:26
  19.5 10.1 %collective-permute-start.5 = (bf16[24,4224]{1,0:T(8,128)(2,1)S(1)}, bf16[24,4224]{1,0:T(8,128)(2,1)S(1)}, u32[]{:S(2)}, u32[]{:S(2)}) collective-permute-start(bf16[24,4224]{1,0:T(8,128)(2,1)S(1)} %pad_maximum_fusion.refs_0_), channel_id=1, source_target_pairs={{0,12},{4,0},{8,4},{12,8},{1,13},{5,1},{9,5},{13,9},{2,14},{6,2},{... | collective-permute-start | bytes 608264 | tf_op jit(solution)/shard_map/ppermute | solution.py:27
  21.5 8.7 %collective-permute-start.4 = (bf16[24,4224]{1,0:T(8,128)(2,1)S(1)}, bf16[24,4224]{1,0:T(8,128)(2,1)S(1)}, u32[]{:S(2)}, u32[]{:S(2)}) collective-permute-start(bf16[24,4224]{1,0:T(8,128)(2,1)S(1)} %pad_maximum_fusion.refs_0_), channel_id=1, source_target_pairs={{0,8},{4,12},{8,0},{12,4},{1,9},{5,13},{9,1},{13,5},{2,10},{6,14},... | collective-permute-start | bytes 608264 | tf_op jit(solution)/shard_map/ppermute | solution.py:27
  23.8 8.5 %collective-permute-start.3 = (bf16[24,4224]{1,0:T(8,128)(2,1)S(1)}, bf16[24,4224]{1,0:T(8,128)(2,1)S(1)}, u32[]{:S(2)}, u32[]{:S(2)}) collective-permute-start(bf16[24,4224]{1,0:T(8,128)(2,1)S(1)} %pad_maximum_fusion.refs_0_), channel_id=1, source_target_pairs={{0,4},{4,8},{8,12},{12,0},{1,5},{5,9},{9,13},{13,1},{2,6},{6,10},{... | collective-permute-start | bytes 608264 | tf_op jit(solution)/shard_map/ppermute | solution.py:27
  25.5 20.1 %collective-permute-start.16 = (bf16[96,2432]{1,0:T(8,128)(2,1)S(1)}, bf16[96,2432]{1,0:T(8,128)(2,1)S(1)}, u32[]{:S(2)}, u32[]{:S(2)}) collective-permute-start(bf16[96,2432]{1,0:T(8,128)(2,1)S(1)} %concatenate.21.refs_0_), channel_id=1, source_target_pairs={{0,48},{16,0},{32,16},{48,32},{1,49},{17,1},{33,17},{49,33},{2,50}... | collective-permute-start | bytes 1400840 | tf_op jit(solution)/shard_map/ppermute | solution.py:27
  27.8 17.8 %collective-permute-start.15 = (bf16[96,2432]{1,0:T(8,128)(2,1)S(1)}, bf16[96,2432]{1,0:T(8,128)(2,1)S(1)}, u32[]{:S(2)}, u32[]{:S(2)}) collective-permute-start(bf16[96,2432]{1,0:T(8,128)(2,1)S(1)} %concatenate.21.refs_0_), channel_id=1, source_target_pairs={{0,32},{16,48},{32,0},{48,16},{1,33},{17,49},{33,1},{49,17},{2,34}... | collective-permute-start | bytes 1400840 | tf_op jit(solution)/shard_map/ppermute | solution.py:27
  29.5 19.8 %collective-permute-start.14 = (bf16[96,2432]{1,0:T(8,128)(2,1)S(1)}, bf16[96,2432]{1,0:T(8,128)(2,1)S(1)}, u32[]{:S(2)}, u32[]{:S(2)}) collective-permute-start(bf16[96,2432]{1,0:T(8,128)(2,1)S(1)} %concatenate.21.refs_0_), channel_id=1, source_target_pairs={{0,16},{16,32},{32,48},{48,0},{1,17},{17,33},{33,49},{49,1},{2,18}... | collective-permute-start | bytes 1400840 | tf_op jit(solution)/shard_map/ppermute | solution.py:27
  35.2 18.4 %collective-permute-start.7 = (bf16[96,4224]{1,0:T(8,128)(2,1)}, bf16[96,4224]{1,0:T(8,128)(2,1)S(1)}, u32[]{:S(2)}, u32[]{:S(2)}) collective-permute-start(bf16[96,4224]{1,0:T(8,128)(2,1)} %stack_kernel.1.refs_0_), channel_id=1, source_target_pairs={{0,66},{2,64},{64,2},{66,0},{1,67},{3,65},{65,3},{67,1},{4,70},{6,... | collective-permute-start | bytes 2433032 | tf_op jit(solution)/shard_map/ppermute | solution.py:26
  38.7 17.9 %collective-permute-start.6 = (bf16[96,4224]{1,0:T(8,128)(2,1)S(1)}, bf16[96,4224]{1,0:T(8,128)(2,1)S(1)}, u32[]{:S(2)}, u32[]{:S(2)}) collective-permute-start(bf16[96,4224]{1,0:T(8,128)(2,1)S(1)} %copy-done.2), channel_id=1, source_target_pairs={{0,64},{2,66},{64,0},{66,2},{1,65},{3,67},{65,1},{67,3},{4,68},{6,... | collective-permute-start | bytes 2433032 | tf_op jit(solution)/shard_map/ppermute | solution.py:26
  45.6 11.9 %collective-permute-start.17 = (bf16[96,2432]{1,0:T(8,128)(2,1)S(1)}, bf16[96,2432]{1,0:T(8,128)(2,1)S(1)}, u32[]{:S(2)}, u32[]{:S(2)}) collective-permute-start(bf16[96,2432]{1,0:T(8,128)(2,1)S(1)} %concatenate.21.refs_0_), channel_id=1, source_target_pairs={{0,1},{1,0},{2,3},{3,2},{4,5},{5,4},{6,7},{7,6},{8,9},{9,8},{10,11... | collective-permute-start | bytes 1400840 | tf_op jit(solution)/shard_map/ppermute | solution.py:21
  45.6 11.9 %collective-permute-start.20 = (bf16[96,2432]{1,0:T(8,128)(2,1)S(1)}, bf16[96,2432]{1,0:T(8,128)(2,1)S(1)}, u32[]{:S(2)}, u32[]{:S(2)}) collective-permute-start(bf16[96,2432]{1,0:T(8,128)(2,1)S(1)} %collective-permute-done.16.refs_3_), channel_id=1, source_target_pairs={{0,1},{1,0},{2,3},{3,2},{4,5},{5,4},{6,7},{7,6},{8,9},{9,8},{10,11... | collective-permute-start | bytes 1400840 | tf_op jit(solution)/shard_map/ppermute | solution.py:21
  56.5 25.6 %collective-permute-start.21 = (bf16[96,4224]{1,0:T(8,128)(2,1)S(1)}, bf16[96,4224]{1,0:T(8,128)(2,1)S(1)}, u32[]{:S(2)}, u32[]{:S(2)}) collective-permute-start(bf16[96,4224]{1,0:T(8,128)(2,1)S(1)} %copy-done.2), channel_id=1, source_target_pairs={{0,2},{2,0},{64,66},{66,64},{1,3},{3,1},{65,67},{67,65},{4,6},{6,4... | collective-permute-start | bytes 2433032 | tf_op jit(solution)/shard_map/ppermute | solution.py:26
  65.4 16.7 %collective-permute-start.22 = (bf16[64,1664]{1,0:T(8,128)(2,1)S(1)}, bf16[64,1664]{1,0:T(8,128)(2,1)S(1)}, u32[]{:S(2)}, u32[]{:S(2)}) collective-permute-start(bf16[64,1664]{1,0:T(8,128)(2,1)S(1)} %get-tuple-element.115), channel_id=1, source_target_pairs={{0,1},{1,2},{2,3},{3,4},{4,5},{5,6},{6,7},{7,8},{8,9},{9,10},{10,1... | collective-permute-start | bytes 638984 | tf_op jit(solution)/shard_map/ppermute | solution.py:561
  68.4 13.8 %collective-permute-start.24 = (bf16[96,4224]{1,0:T(8,128)(2,1)S(1)}, bf16[96,4224]{1,0:T(8,128)(2,1)S(1)}, u32[]{:S(2)}, u32[]{:S(2)}) collective-permute-start(bf16[96,4224]{1,0:T(8,128)(2,1)S(1)} %copy-done.2), channel_id=1, source_target_pairs={{0,1},{1,0},{2,3},{3,2},{4,5},{5,4},{6,7},{7,6},{8,9},{9,8},{10,11... | collective-permute-start | bytes 2433032 | tf_op jit(solution)/shard_map/ppermute | solution.py:21
  71.4 10.7 %collective-permute-start.26 = (bf16[96,4224]{1,0:T(8,128)(2,1)S(1)}, bf16[96,4224]{1,0:T(8,128)(2,1)S(1)}, u32[]{:S(2)}, u32[]{:S(2)}) collective-permute-start(bf16[96,4224]{1,0:T(8,128)(2,1)S(1)} %collective-permute-done.6.refs_2_), channel_id=1, source_target_pairs={{0,1},{1,0},{2,3},{3,2},{4,5},{5,4},{6,7},{7,6},{8,9},{9,8},{10,11... | collective-permute-start | bytes 2433032 | tf_op jit(solution)/shard_map/ppermute | solution.py:21
  71.5 12.5 %collective-permute-start.27 = (bf16[96,4224]{1,0:T(8,128)(2,1)S(1)}, bf16[96,4224]{1,0:T(8,128)(2,1)S(1)}, u32[]{:S(2)}, u32[]{:S(2)}) collective-permute-start(bf16[96,4224]{1,0:T(8,128)(2,1)S(1)} %collective-permute-done.7.refs_3_), channel_id=1, source_target_pairs={{0,1},{1,0},{2,3},{3,2},{4,5},{5,4},{6,7},{7,6},{8,9},{9,8},{10,11... | collective-permute-start | bytes 2433032 | tf_op jit(solution)/shard_map/ppermute | solution.py:21
  108.1 22.6 %collective-permute-start.28 = (bf16[384,4224]{1,0:T(8,128)(2,1)}, bf16[384,4224]{1,0:T(8,128)(2,1)S(1)}, u32[]{:S(2)}, u32[]{:S(2)}) collective-permute-start(bf16[384,4224]{1,0:T(8,128)(2,1)} %get-tuple-element.79), channel_id=1, source_target_pairs={{0,1},{1,0},{2,3},{3,2},{4,5},{5,4},{6,7},{7,6},{8,9},{9,8},{10,11... | collective-permute-start | bytes 9732104 | tf_op jit(solution)/shard_map/ppermute | solution.py:21
  127.3 8.8 %collective-permute-start.29 = (bf16[64,1536]{1,0:T(8,128)(2,1)S(1)}, bf16[64,1536]{1,0:T(8,128)(2,1)S(1)}, u32[]{:S(2)}, u32[]{:S(2)}) collective-permute-start(bf16[64,1536]{1,0:T(8,128)(2,1)S(1)} %get-tuple-element.83), channel_id=1, source_target_pairs={{0,1},{1,2},{2,3},{3,4},{4,5},{5,6},{6,7},{7,8},{8,9},{9,10},{10,1... | collective-permute-start | bytes 589832 | tf_op jit(solution)/shard_map/ppermute | solution.py:612
  136.1 18.7 %collective-permute-start.31 = (bf16[96,4224]{1,0:T(8,128)(2,1)S(1)}, bf16[96,4224]{1,0:T(8,128)(2,1)S(1)}, u32[]{:S(2)}, u32[]{:S(2)}) collective-permute-start(bf16[96,4224]{1,0:T(8,128)(2,1)S(1)} %get-tuple-element.86), channel_id=1, source_target_pairs={{0,64},{2,66},{64,0},{66,2},{1,65},{3,67},{65,1},{67,3},{4,68},{6,... | collective-permute-start | bytes 2433032 | tf_op jit(solution)/shard_map/ppermute | solution.py:26
  136.5 23.9 %collective-permute-start.32 = (bf16[96,4224]{1,0:T(8,128)(2,1)S(1)}, bf16[96,4224]{1,0:T(8,128)(2,1)S(1)}, u32[]{:S(2)}, u32[]{:S(2)}) collective-permute-start(bf16[96,4224]{1,0:T(8,128)(2,1)S(1)} %get-tuple-element.87), channel_id=1, source_target_pairs={{0,66},{2,64},{64,2},{66,0},{1,67},{3,65},{65,3},{67,1},{4,70},{6,... | collective-permute-start | bytes 2433032 | tf_op jit(solution)/shard_map/ppermute | solution.py:26
  150.4 10.0 %collective-permute-start.33 = (bf16[96,2432]{1,0:T(8,128)(2,1)S(1)}, bf16[96,2432]{1,0:T(8,128)(2,1)S(1)}, u32[]{:S(2)}, u32[]{:S(2)}) collective-permute-start(bf16[96,2432]{1,0:T(8,128)(2,1)S(1)} %get-tuple-element.96), channel_id=1, source_target_pairs={{0,1},{1,0},{2,3},{3,2},{4,5},{5,4},{6,7},{7,6},{8,9},{9,8},{10,11... | collective-permute-start | bytes 1400840 | tf_op jit(solution)/shard_map/ppermute | solution.py:21
  150.5 9.9 %collective-permute-start.34 = (bf16[96,2432]{1,0:T(8,128)(2,1)S(1)}, bf16[96,2432]{1,0:T(8,128)(2,1)S(1)}, u32[]{:S(2)}, u32[]{:S(2)}) collective-permute-start(bf16[96,2432]{1,0:T(8,128)(2,1)S(1)} %get-tuple-element.97), channel_id=1, source_target_pairs={{0,1},{1,0},{2,3},{3,2},{4,5},{5,4},{6,7},{7,6},{8,9},{9,8},{10,11... | collective-permute-start | bytes 1400840 | tf_op jit(solution)/shard_map/ppermute | solution.py:21
  151.0 9.4 %collective-permute-start.35 = (bf16[96,2432]{1,0:T(8,128)(2,1)S(1)}, bf16[96,2432]{1,0:T(8,128)(2,1)S(1)}, u32[]{:S(2)}, u32[]{:S(2)}) collective-permute-start(bf16[96,2432]{1,0:T(8,128)(2,1)S(1)} %get-tuple-element.98), channel_id=1, source_target_pairs={{0,1},{1,0},{2,3},{3,2},{4,5},{5,4},{6,7},{7,6},{8,9},{9,8},{10,11... | collective-permute-start | bytes 1400840 | tf_op jit(solution)/shard_map/ppermute | solution.py:21
  162.4 13.7 %collective-permute-start.37 = (bf16[96,2432]{1,0:T(8,128)(2,1)S(1)}, bf16[96,2432]{1,0:T(8,128)(2,1)S(1)}, u32[]{:S(2)}, u32[]{:S(2)}) collective-permute-start(bf16[96,2432]{1,0:T(8,128)(2,1)S(1)} %get-tuple-element.101), channel_id=1, source_target_pairs={{0,48},{16,0},{32,16},{48,32},{1,49},{17,1},{33,17},{49,33},{2,50}... | collective-permute-start | bytes 1400840 | tf_op jit(solution)/shard_map/ppermute | solution.py:27
  164.4 15.2 %collective-permute-start.38 = (bf16[96,2432]{1,0:T(8,128)(2,1)S(1)}, bf16[96,2432]{1,0:T(8,128)(2,1)S(1)}, u32[]{:S(2)}, u32[]{:S(2)}) collective-permute-start(bf16[96,2432]{1,0:T(8,128)(2,1)S(1)} %get-tuple-element.102), channel_id=1, source_target_pairs={{0,32},{16,48},{32,0},{48,16},{1,33},{17,49},{33,1},{49,17},{2,34}... | collective-permute-start | bytes 1400840 | tf_op jit(solution)/shard_map/ppermute | solution.py:27
  165.3 22.1 %collective-permute-start.39 = (bf16[96,2432]{1,0:T(8,128)(2,1)S(1)}, bf16[96,2432]{1,0:T(8,128)(2,1)S(1)}, u32[]{:S(2)}, u32[]{:S(2)}) collective-permute-start(bf16[96,2432]{1,0:T(8,128)(2,1)S(1)} %get-tuple-element.103), channel_id=1, source_target_pairs={{0,16},{16,32},{32,48},{48,0},{1,17},{17,33},{33,49},{49,1},{2,18}... | collective-permute-start | bytes 1400840 | tf_op jit(solution)/shard_map/ppermute | solution.py:27
  166.5 26.8 %collective-permute-start.43 = (bf16[96,4224]{1,0:T(8,128)(2,1)S(1)}, bf16[96,4224]{1,0:T(8,128)(2,1)S(1)}, u32[]{:S(2)}, u32[]{:S(2)}) collective-permute-start(bf16[96,4224]{1,0:T(8,128)(2,1)S(1)} %get-tuple-element.105), channel_id=1, source_target_pairs={{0,2},{2,0},{64,66},{66,64},{1,3},{3,1},{65,67},{67,65},{4,6},{6,4... | collective-permute-start | bytes 2433032 | tf_op jit(solution)/shard_map/ppermute | solution.py:26
  187.7 8.9 %collective-permute-start.40 = (bf16[24,2432]{1,0:T(8,128)(2,1)S(1)}, bf16[24,2432]{1,0:T(8,128)(2,1)S(1)}, u32[]{:S(2)}, u32[]{:S(2)}) collective-permute-start(bf16[24,2432]{1,0:T(8,128)(2,1)S(1)} %get-tuple-element.119), channel_id=1, source_target_pairs={{0,2},{2,0},{64,66},{66,64},{1,3},{3,1},{65,67},{67,65},{4,6},{6,4... | collective-permute-start | bytes 350216 | tf_op jit(solution)/shard_map/ppermute | solution.py:26
  193.6 8.8 %collective-permute-start.44 = (bf16[24,4224]{1,0:T(8,128)(2,1)S(1)}, bf16[24,4224]{1,0:T(8,128)(2,1)S(1)}, u32[]{:S(2)}, u32[]{:S(2)}) collective-permute-start(bf16[24,4224]{1,0:T(8,128)(2,1)S(1)} %get-tuple-element.116), channel_id=1, source_target_pairs={{0,12},{4,0},{8,4},{12,8},{1,13},{5,1},{9,5},{13,9},{2,14},{6,2},{... | collective-permute-start | bytes 608264 | tf_op jit(solution)/shard_map/ppermute | solution.py:27
  196.5 11.4 %collective-permute-start.45 = (bf16[24,4224]{1,0:T(8,128)(2,1)S(1)}, bf16[24,4224]{1,0:T(8,128)(2,1)S(1)}, u32[]{:S(2)}, u32[]{:S(2)}) collective-permute-start(bf16[24,4224]{1,0:T(8,128)(2,1)S(1)} %get-tuple-element.118), channel_id=1, source_target_pairs={{0,8},{4,12},{8,0},{12,4},{1,9},{5,13},{9,1},{13,5},{2,10},{6,14},... | collective-permute-start | bytes 608264 | tf_op jit(solution)/shard_map/ppermute | solution.py:27
  (36 other events, 223.6 us)

commit v2 on v1

--- a/solution.py
+++ b/solution.py
@@ -115,17 +115,19 @@
 def project_kernel(*refs):
     pieces = refs[:8]
     tokens, choose, cosine, sine, marks = refs[8:13]
-    queries, key_values, ordered, gains, kept, weight, sems, out_sems = refs[13:]
+    queries, key_values, ordered, gains, kept, weight, gain_cols, gain_sems, sems, out_sems = refs[13:]
+    gain_copies = load_pieces(pieces, gain_cols, gain_sems, 2304)
     copies = load_pieces(pieces, weight, sems, 0)
     unit, _ = normed(tokens[...].astype(F32))
-    wait_all(copies)
-    sent = send_out(weight, kept, out_sems.at[0])
-    gain_order = dot_nt(unit_rows(), weight[:, 2304:]).astype(BF16)
+    wait_all(gain_copies)
+    gain_order = dot_nt(unit_rows(), gain_cols[...]).astype(BF16)
     gain = dot_nt(gain_order, choose[...])
     gains[...] = gain
     h_one = (unit * gain[0:1]).astype(BF16)
     h_ord = dot(h_one, choose[...]).astype(BF16)
     ordered[...] = h_ord
+    wait_all(copies)
+    sent = send_out(weight, kept, out_sems.at[0])
     cos_w, sin_w = wide(cosine[...], 6), wide(sine[...], 6)
     part = dot(h_ord, weight[:, :768])
     queries[...] = (rotate(part, cos_w, sin_w) * 0.125).astype(BF16)
@@ -401,7 +403,7 @@
         in_specs=[pl.BlockSpec(memory_space=pl.ANY)] * len(pieces) + [whole] * len(args),
         out_specs=[far if isinstance(shape, list) else whole for shape, _ in outs],
         scratch_shapes=[pltpu.VMEM(shape, dtype) for shape, dtype in scratch]
-        + [pltpu.SemaphoreType.DMA((max(len(pieces), 1),))] * (2 if out_copies == 6 else len(pieces) // 8)
+        + [pltpu.SemaphoreType.DMA((max(len(pieces), 1),))] * (2 if out_copies in (1, 6) else len(pieces) // 8)
         + [pltpu.SemaphoreType.DMA((out_copies,))] * (out_copies > 0),
         compiler_params=pltpu.CompilerParams(vmem_limit_bytes=48 * 1024 * 1024),
         cost_estimate=pl.CostEstimate(
@@ -544,7 +546,7 @@
             ((256, 1664), BF16),
             ((256, 768), BF16),
             ((8, 768), F32),
-            ([768, 2432], BF16),
+            ([768, 2304], BF16),
         ],
         pieces_a,
         (
@@ -555,7 +557,7 @@
             marks,
         ),
         4e9,
-        [((768, 2432), BF16)],
+        [((768, 2304), BF16), ((768, 128), BF16)],
         1,
     )
     prev = lax.ppermute(key_values[192:], SEQ, next_pairs(1))

time: 225 us -> 225 us (level)
  transfers between devices with their start and end apart: 53 -> 53, of which waited for: 20 -> 20; matrix products, arithmetic and copies ran while one was open for 6% -> 6% of each run, Pallas kernels for 14% -> 13%
where the time goes in v2:
time: 225 us; the launch traced here: 221 us
  starting transfers between devices  94.4 us (42%)
  Pallas kernels  52.8 us (23%)
  waiting for transfers between devices  52.1 us (23%)
  other arithmetic  11.7 us (5%)
  local copies, waits for them, and re-layouts  8.96 us (4%)
    pallas_call x5, Pallas kernels, call(): pl.pallas_call(kernel, out_shape=shapes, in_specs=[pl.BlockSpec(memory_sp...  45 us
    ppermute x24, waiting for transfers between devices, line_send(): return lax.ppermute(value, axis, [(i, (i + step) % 4) for i in range(4)])  36.3 us
    ppermute x24, starting transfers between devices, line_send(): return lax.ppermute(value, axis, [(i, (i + step) % 4) for i in range(4)])  35.5 us
    ppermute x13, starting transfers between devices, swap_cores(): return lax.ppermute(value, 'core', [(0, 1), (1, 0)])  28.3 us
    ppermute x12, starting transfers between devices, line_send(): return lax.ppermute(value, X, [(i, i ^ step) for i in range(4)])  22.9 us
    ppermute x12, waiting for transfers between devices, line_send(): return lax.ppermute(value, X, [(i, i ^ step) for i in range(4)])  12.7 us
    convert_element_type x4, other arithmetic, chooser(): (jnp.arange(count, dtype=jnp.int32)[:, None] == natural[None, :]).astype(...  6.85 us
    unnamed x30, local copies, waits for them, and re-layouts  4.86 us
  transfers between devices with their start and end apart: 53, of which 20 were waited for; matrix products, arithmetic and copies ran while one was open for 6% of the time, Pallas kernels for 13%

profile of v2, /device:TPU:2, one launch (start us, length us, event | category | flops | bytes accessed | tf_op | source)
XLA Modules:
  0.0 221.2 jit_solution(1178920181498198846)
XLA Ops:
  2.2 4.0 %collective-permute-start.10 = (bf16[6,2432]{1,0:T(8,128)(2,1)}, bf16[6,2432]{1,0:T(8,128)(2,1)S(1)}, u32[]{:S(2)}, u32[]{:S(2)}) collective-permute-start(bf16[6,2432]{1,0:T(8,128)(2,1)} %get-tuple-element.59), channel_id=1, source_target_pairs={{0,12},{4,0},{8,4},{12,8},{1,13},{5,1},{9,5},{13,9},{2,14},{6,2},{... | collective-permute-start | bytes 87560 | tf_op jit(solution)/shard_map/ppermute | solution.py:27
  7.5 3.0 %collective-permute-start.2 = (bf16[6,4224]{1,0:T(8,128)(2,1)}, bf16[6,4224]{1,0:T(8,128)(2,1)S(1)}, u32[]{:S(2)}, u32[]{:S(2)}) collective-permute-start(bf16[6,4224]{1,0:T(8,128)(2,1)} %get-tuple-element.58), channel_id=1, source_target_pairs={{0,48},{16,0},{32,16},{48,32},{1,49},{17,1},{33,17},{49,33},{2,50}... | collective-permute-start | bytes 152072 | tf_op jit(solution)/shard_map/ppermute | solution.py:27
  19.5 2.0 collective-permute-start.5
  21.5 2.3 %collective-permute-start.4 = (bf16[24,4224]{1,0:T(8,128)(2,1)S(1)}, bf16[24,4224]{1,0:T(8,128)(2,1)S(1)}, u32[]{:S(2)}, u32[]{:S(2)}) collective-permute-start(bf16[24,4224]{1,0:T(8,128)(2,1)S(1)} %pad_maximum_fusion.refs_0_), channel_id=1, source_target_pairs={{0,8},{4,12},{8,0},{12,4},{1,9},{5,13},{9,1},{13,5},{2,10},{6,14},... | collective-permute-start | bytes 608264 | tf_op jit(solution)/shard_map/ppermute | solution.py:27
  25.5 2.3 %collective-permute-start.16 = (bf16[96,2432]{1,0:T(8,128)(2,1)S(1)}, bf16[96,2432]{1,0:T(8,128)(2,1)S(1)}, u32[]{:S(2)}, u32[]{:S(2)}) collective-permute-start(bf16[96,2432]{1,0:T(8,128)(2,1)S(1)} %concatenate.21.refs_0_), channel_id=1, source_target_pairs={{0,48},{16,0},{32,16},{48,32},{1,49},{17,1},{33,17},{49,33},{2,50}... | collective-permute-start | bytes 1400840 | tf_op jit(solution)/shard_map/ppermute | solution.py:27
  30.2 2.1 collective-permute-done.3.refs_1_
  33.0 2.2 stack_kernel.1.refs_0_
  46.1 3.2 %collective-permute-done.14.refs_1_ = bf16[96,2432]{1,0:T(8,128)(2,1)S(1)} collective-permute-done((bf16[96,2432]{1,0:T(8,128)(2,1)S(1)}, bf16[96,2432]{1,0:T(8,128)(2,1)S(1)}, u32[]{:S(2)}, u32[]{:S(2)}) %collective-permute-start.14) | collective-permute-done | bytes 466976 | tf_op jit(solution)/shard_map/ppermute | solution.py:27
  49.3 4.2 %collective-permute-done.7.refs_3_ = bf16[96,4224]{1,0:T(8,128)(2,1)S(1)} collective-permute-done((bf16[96,4224]{1,0:T(8,128)(2,1)}, bf16[96,4224]{1,0:T(8,128)(2,1)S(1)}, u32[]{:S(2)}, u32[]{:S(2)}) %collective-permute-start.7) | collective-permute-done | bytes 811040 | tf_op jit(solution)/shard_map/ppermute | solution.py:26
  57.6 4.7 %project_kernel.1 = (bf16[256,768]{1,0:T(8,128)(2,1)S(1)}, bf16[256,1664]{1,0:T(8,128)(2,1)S(1)}, bf16[256,768]{1,0:T(8,128)(2,1)S(1)}, f32[8,768]{1,0:T(8,128)S(1)}, bf16[768,2304]{1,0:T(8,128)(2,1)}) custom-call(bf16[96,2432]{1,0:T(8,128)(2,1)S(1)} %concatenate.21.refs_0_, bf16[96,2432]{1,0:T(8,128)(2,1)S(1)} %collective-permute-done.14.refs_1_, ...), custom_call_target="tpu_custom_call" | custom-call | flops 4000000000 | bytes 10838016 | tf_op jit(solution)/shard_map/project_kernel/pallas_call | solution.py:400
  63.7 3.0 %collective-permute-start.22 = (bf16[64,1664]{1,0:T(8,128)(2,1)S(1)}, bf16[64,1664]{1,0:T(8,128)(2,1)S(1)}, u32[]{:S(2)}, u32[]{:S(2)}) collective-permute-start(bf16[64,1664]{1,0:T(8,128)(2,1)S(1)} %get-tuple-element.115), channel_id=1, source_target_pairs={{0,1},{1,2},{2,3},{3,4},{4,5},{5,6},{6,7},{7,8},{8,9},{9,10},{10,1... | collective-permute-start | bytes 638984 | tf_op jit(solution)/shard_map/ppermute | solution.py:563
  66.8 3.0 %collective-permute-start.24 = (bf16[96,4224]{1,0:T(8,128)(2,1)S(1)}, bf16[96,4224]{1,0:T(8,128)(2,1)S(1)}, u32[]{:S(2)}, u32[]{:S(2)}) collective-permute-start(bf16[96,4224]{1,0:T(8,128)(2,1)S(1)} %copy-done.2), channel_id=1, source_target_pairs={{0,1},{1,0},{2,3},{3,2},{4,5},{5,4},{6,7},{7,6},{8,9},{9,8},{10,11... | collective-permute-start | bytes 2433032 | tf_op jit(solution)/shard_map/ppermute | solution.py:21
  69.9 12.2 %collective-permute-start.27 = (bf16[96,4224]{1,0:T(8,128)(2,1)S(1)}, bf16[96,4224]{1,0:T(8,128)(2,1)S(1)}, u32[]{:S(2)}, u32[]{:S(2)}) collective-permute-start(bf16[96,4224]{1,0:T(8,128)(2,1)S(1)} %collective-permute-done.7.refs_3_), channel_id=1, source_target_pairs={{0,1},{1,0},{2,3},{3,2},{4,5},{5,4},{6,7},{7,6},{8,9},{9,8},{10,11... | collective-permute-start | bytes 2433032 | tf_op jit(solution)/shard_map/ppermute | solution.py:21
  86.1 5.4 %attend_kernel.1 = (bf16[256,768]{1,0:T(8,128)(2,1)S(1)}, f32[256,768]{1,0:T(8,128)S(1)}, bf16[12,256,256]{2,1,0:T(8,128)(2,1)}) custom-call(bf16[96,4224]{1,0:T(8,128)(2,1)S(1)} %copy-done.2, bf16[96,4224]{1,0:T(8,128)(2,1)S(1)} %collective-permute-done.21.refs_1_, bf16[96,4224]{1,0:T(8,128)(2,1)S(1)} %collective-permute-done.6.refs_2_, ...), custom_call_target="tpu_custom_call" | custom-call | flops 4000000000 | bytes 12484608 | tf_op jit(solution)/shard_map/attend_kernel/pallas_call | solution.py:400
  91.6 16.6 %feed_kernel.1 = (bf16[256,768]{1,0:T(8,128)(2,1)}, bf16[384,4224]{1,0:T(8,128)(2,1)}, bf16[384,4224]{1,0:T(8,128)(2,1)}, f32[256,768]{1,0:T(8,128)S(1)}, f32[8,768]{1,0:T(8,128)S(1)}) custom-call(bf16[96,4224]{1,0:T(8,128)(2,1)S(1)} %copy-done.2, bf16[96,4224]{1,0:T(8,128)(2,1)S(1)} %collective-permute-done.21.refs_1_, ...), custom_call_target="tpu_custom_call" | custom-call | flops 15000000512 | bytes 20496384 | tf_op jit(solution)/shard_map/feed_kernel/pallas_call | solution.py:400
  108.2 9.2 %collective-permute-start.28 = (bf16[384,4224]{1,0:T(8,128)(2,1)}, bf16[384,4224]{1,0:T(8,128)(2,1)S(1)}, u32[]{:S(2)}, u32[]{:S(2)}) collective-permute-start(bf16[384,4224]{1,0:T(8,128)(2,1)} %get-tuple-element.79), channel_id=1, source_target_pairs={{0,1},{1,0},{2,3},{3,2},{4,5},{5,4},{6,7},{7,6},{8,9},{9,8},{10,11... | collective-permute-start | bytes 9732104 | tf_op jit(solution)/shard_map/ppermute | solution.py:21
  117.4 10.0 %attend_back_kernel.1 = (bf16[256,768]{1,0:T(8,128)(2,1)S(1)}, f32[256,1536]{1,0:T(8,128)}, bf16[64,1536]{1,0:T(8,128)(2,1)S(1)}, bf16[64,1536]{1,0:T(8,128)(2,1)S(1)}) custom-call(bf16[96,4224]{1,0:T(8,128)(2,1)S(1)} %copy-done.2, bf16[96,4224]{1,0:T(8,128)(2,1)S(1)} %collective-permute-done.21.refs_1_, ...), custom_call_target="tpu_custom_call" | custom-call | flops 10000000000 | bytes 14319616 | tf_op jit(solution)/shard_map/attend_back_kernel/pallas_call | solution.py:400
  132.5 3.6 %fold_kernel.2 = (f32[96,4224]{1,0:T(8,128)S(1)}, bf16[96,4224]{1,0:T(8,128)(2,1)S(1)}, bf16[96,4224]{1,0:T(8,128)(2,1)S(1)}, bf16[96,4224]{1,0:T(8,128)(2,1)S(1)}) custom-call(bf16[384,4224]{1,0:T(8,128)(2,1)} %get-tuple-element.78.own, bf16[384,4224]{1,0:T(8,128)(2,1)} %copy-done.6), custom_call_target="tpu_custom_call" | custom-call | flops 1 | bytes 1 | tf_op jit(solution)/shard_map/fold_kernel/pallas_call | solution.py:465
  136.6 5.5 %collective-permute-start.32 = (bf16[96,4224]{1,0:T(8,128)(2,1)S(1)}, bf16[96,4224]{1,0:T(8,128)(2,1)S(1)}, u32[]{:S(2)}, u32[]{:S(2)}) collective-permute-start(bf16[96,4224]{1,0:T(8,128)(2,1)S(1)} %get-tuple-element.87), channel_id=1, source_target_pairs={{0,66},{2,64},{64,2},{66,0},{1,67},{3,65},{65,3},{67,1},{4,70},{6,... | collective-permute-start | bytes 2433032 | tf_op jit(solution)/shard_map/ppermute | solution.py:26
  142.1 8.2 %project_back_kernel.1 = (bf16[256,768]{1,0:T(8,128)(2,1)}, bf16[384,2432]{1,0:T(8,128)(2,1)}, bf16[96,2432]{1,0:T(8,128)(2,1)S(1)}, bf16[96,2432]{1,0:T(8,128)(...) custom-call(bf16[256,768]{1,0:T(8,128)(2,1)S(1)} %get-tuple-element.88.refs_0_, ...), custom_call_target="tpu_custom_call" | custom-call | flops 1 | bytes 1 | tf_op jit(solution)/shard_map/project_back_kernel/pallas_call | solution.py:400
  151.1 3.8 %collective-permute-done.31 = bf16[96,4224]{1,0:T(8,128)(2,1)S(1)} collective-permute-done((bf16[96,4224]{1,0:T(8,128)(2,1)S(1)}, bf16[96,4224]{1,0:T(8,128)(2,1)S(1)}, u32[]{:S(2)}, u32[]{:S(2)}) %collective-permute-start.31) | collective-permute-done | bytes 811040 | tf_op jit(solution)/shard_map/ppermute | solution.py:26
  154.9 2.4 %collective-permute-start.36 = (bf16[96,2432]{1,0:T(8,128)(2,1)S(1)}, bf16[96,2432]{1,0:T(8,128)(2,1)S(1)}, u32[]{:S(2)}, u32[]{:S(2)}) collective-permute-start(bf16[96,2432]{1,0:T(8,128)(2,1)S(1)} %get-tuple-element.99), channel_id=1, source_target_pairs={{0,1},{1,0},{2,3},{3,2},{4,5},{5,4},{6,7},{7,6},{8,9},{9,8},{10,11... | collective-permute-start | bytes 1400840 | tf_op jit(solution)/shard_map/ppermute | solution.py:21
  157.3 3.1 %collective-permute-done.32 = bf16[96,4224]{1,0:T(8,128)(2,1)S(1)} collective-permute-done((bf16[96,4224]{1,0:T(8,128)(2,1)S(1)}, bf16[96,4224]{1,0:T(8,128)(2,1)S(1)}, u32[]{:S(2)}, u32[]{:S(2)}) %collective-permute-start.32) | collective-permute-done | bytes 811040 | tf_op jit(solution)/shard_map/ppermute | solution.py:26
  166.5 3.5 %collective-permute-start.43 = (bf16[96,4224]{1,0:T(8,128)(2,1)S(1)}, bf16[96,4224]{1,0:T(8,128)(2,1)S(1)}, u32[]{:S(2)}, u32[]{:S(2)}) collective-permute-start(bf16[96,4224]{1,0:T(8,128)(2,1)S(1)} %get-tuple-element.105), channel_id=1, source_target_pairs={{0,2},{2,0},{64,66},{66,64},{1,3},{3,1},{65,67},{67,65},{4,6},{6,4... | collective-permute-start | bytes 2433032 | tf_op jit(solution)/shard_map/ppermute | solution.py:26
  170.0 6.1 %collective-permute-done.37 = bf16[96,2432]{1,0:T(8,128)(2,1)S(1)} collective-permute-done((bf16[96,2432]{1,0:T(8,128)(2,1)S(1)}, bf16[96,2432]{1,0:T(8,128)(2,1)S(1)}, u32[]{:S(2)}, u32[]{:S(2)}) %collective-permute-start.37) | collective-permute-done | bytes 466976 | tf_op jit(solution)/shard_map/ppermute | solution.py:27
  176.1 3.5 %collective-permute-done.38 = bf16[96,2432]{1,0:T(8,128)(2,1)S(1)} collective-permute-done((bf16[96,2432]{1,0:T(8,128)(2,1)S(1)}, bf16[96,2432]{1,0:T(8,128)(2,1)S(1)}, u32[]{:S(2)}, u32[]{:S(2)}) %collective-permute-start.38) | collective-permute-done | bytes 466976 | tf_op jit(solution)/shard_map/ppermute | solution.py:27
  179.6 7.9 %collective-permute-done.39 = bf16[96,2432]{1,0:T(8,128)(2,1)S(1)} collective-permute-done((bf16[96,2432]{1,0:T(8,128)(2,1)S(1)}, bf16[96,2432]{1,0:T(8,128)(2,1)S(1)}, u32[]{:S(2)}, u32[]{:S(2)}) %collective-permute-start.39) | collective-permute-done | bytes 466976 | tf_op jit(solution)/shard_map/ppermute | solution.py:27
  187.8 4.2 %collective-permute-start.40 = (bf16[24,2432]{1,0:T(8,128)(2,1)S(1)}, bf16[24,2432]{1,0:T(8,128)(2,1)S(1)}, u32[]{:S(2)}, u32[]{:S(2)}) collective-permute-start(bf16[24,2432]{1,0:T(8,128)(2,1)S(1)} %get-tuple-element.119), channel_id=1, source_target_pairs={{0,2},{2,0},{64,66},{66,64},{1,3},{3,1},{65,67},{67,65},{4,6},{6,4... | collective-permute-start | bytes 350216 | tf_op jit(solution)/shard_map/ppermute | solution.py:26
  193.7 2.0 collective-permute-start.44
  196.6 3.7 %collective-permute-start.45 = (bf16[24,4224]{1,0:T(8,128)(2,1)S(1)}, bf16[24,4224]{1,0:T(8,128)(2,1)S(1)}, u32[]{:S(2)}, u32[]{:S(2)}) collective-permute-start(bf16[24,4224]{1,0:T(8,128)(2,1)S(1)} %get-tuple-element.118), channel_id=1, source_target_pairs={{0,8},{4,12},{8,0},{12,4},{1,9},{5,13},{9,1},{13,5},{2,10},{6,14},... | collective-permute-start | bytes 608264 | tf_op jit(solution)/shard_map/ppermute | solution.py:27
  200.4 2.1 collective-permute-done.44
  204.0 4.0 %collective-permute-done.45 = bf16[24,4224]{1,0:T(8,128)(2,1)S(1)} collective-permute-done((bf16[24,4224]{1,0:T(8,128)(2,1)S(1)}, bf16[24,4224]{1,0:T(8,128)(2,1)S(1)}, u32[]{:S(2)}, u32[]{:S(2)}) %collective-permute-start.45) | collective-permute-done | bytes 202784 | tf_op jit(solution)/shard_map/ppermute | solution.py:27
  (148 shorter events, 66.3 us)
Async XLA Ops:
  2.2 10.5 %collective-permute-start.10 = (bf16[6,2432]{1,0:T(8,128)(2,1)}, bf16[6,2432]{1,0:T(8,128)(2,1)S(1)}, u32[]{:S(2)}, u32[]{:S(2)}) collective-permute-start(bf16[6,2432]{1,0:T(8,128)(2,1)} %get-tuple-element.59), channel_id=1, source_target_pairs={{0,12},{4,0},{8,4},{12,8},{1,13},{5,1},{9,5},{13,9},{2,14},{6,2},{... | collective-permute-start | bytes 87560 | tf_op jit(solution)/shard_map/ppermute | solution.py:27
  7.5 10.5 %collective-permute-start.2 = (bf16[6,4224]{1,0:T(8,128)(2,1)}, bf16[6,4224]{1,0:T(8,128)(2,1)S(1)}, u32[]{:S(2)}, u32[]{:S(2)}) collective-permute-start(bf16[6,4224]{1,0:T(8,128)(2,1)} %get-tuple-element.58), channel_id=1, source_target_pairs={{0,48},{16,0},{32,16},{48,32},{1,49},{17,1},{33,17},{49,33},{2,50}... | collective-permute-start | bytes 152072 | tf_op jit(solution)/shard_map/ppermute | solution.py:27
  14.6 9.3 %collective-permute-start.13 = (bf16[24,2432]{1,0:T(8,128)(2,1)S(1)}, bf16[24,2432]{1,0:T(8,128)(2,1)S(1)}, u32[]{:S(2)}, u32[]{:S(2)}) collective-permute-start(bf16[24,2432]{1,0:T(8,128)(2,1)S(1)} %pad_maximum_fusion.3), channel_id=1, source_target_pairs={{0,66},{2,64},{64,2},{66,0},{1,67},{3,65},{65,3},{67,1},{4,70},{6,... | collective-permute-start | bytes 350216 | tf_op jit(solution)/shard_map/ppermute | solution.py:26
  19.5 10.1 %collective-permute-start.5 = (bf16[24,4224]{1,0:T(8,128)(2,1)S(1)}, bf16[24,4224]{1,0:T(8,128)(2,1)S(1)}, u32[]{:S(2)}, u32[]{:S(2)}) collective-permute-start(bf16[24,4224]{1,0:T(8,128)(2,1)S(1)} %pad_maximum_fusion.refs_0_), channel_id=1, source_target_pairs={{0,12},{4,0},{8,4},{12,8},{1,13},{5,1},{9,5},{13,9},{2,14},{6,2},{... | collective-permute-start | bytes 608264 | tf_op jit(solution)/shard_map/ppermute | solution.py:27
  21.5 8.7 %collective-permute-start.4 = (bf16[24,4224]{1,0:T(8,128)(2,1)S(1)}, bf16[24,4224]{1,0:T(8,128)(2,1)S(1)}, u32[]{:S(2)}, u32[]{:S(2)}) collective-permute-start(bf16[24,4224]{1,0:T(8,128)(2,1)S(1)} %pad_maximum_fusion.refs_0_), channel_id=1, source_target_pairs={{0,8},{4,12},{8,0},{12,4},{1,9},{5,13},{9,1},{13,5},{2,10},{6,14},... | collective-permute-start | bytes 608264 | tf_op jit(solution)/shard_map/ppermute | solution.py:27
  23.8 8.5 %collective-permute-start.3 = (bf16[24,4224]{1,0:T(8,128)(2,1)S(1)}, bf16[24,4224]{1,0:T(8,128)(2,1)S(1)}, u32[]{:S(2)}, u32[]{:S(2)}) collective-permute-start(bf16[24,4224]{1,0:T(8,128)(2,1)S(1)} %pad_maximum_fusion.refs_0_), channel_id=1, source_target_pairs={{0,4},{4,8},{8,12},{12,0},{1,5},{5,9},{9,13},{13,1},{2,6},{6,10},{... | collective-permute-start | bytes 608264 | tf_op jit(solution)/shard_map/ppermute | solution.py:27
  25.5 20.1 %collective-permute-start.16 = (bf16[96,2432]{1,0:T(8,128)(2,1)S(1)}, bf16[96,2432]{1,0:T(8,128)(2,1)S(1)}, u32[]{:S(2)}, u32[]{:S(2)}) collective-permute-start(bf16[96,2432]{1,0:T(8,128)(2,1)S(1)} %concatenate.21.refs_0_), channel_id=1, source_target_pairs={{0,48},{16,0},{32,16},{48,32},{1,49},{17,1},{33,17},{49,33},{2,50}... | collective-permute-start | bytes 1400840 | tf_op jit(solution)/shard_map/ppermute | solution.py:27
  27.8 17.8 %collective-permute-start.15 = (bf16[96,2432]{1,0:T(8,128)(2,1)S(1)}, bf16[96,2432]{1,0:T(8,128)(2,1)S(1)}, u32[]{:S(2)}, u32[]{:S(2)}) collective-permute-start(bf16[96,2432]{1,0:T(8,128)(2,1)S(1)} %concatenate.21.refs_0_), channel_id=1, source_target_pairs={{0,32},{16,48},{32,0},{48,16},{1,33},{17,49},{33,1},{49,17},{2,34}... | collective-permute-start | bytes 1400840 | tf_op jit(solution)/shard_map/ppermute | solution.py:27
  29.5 19.8 %collective-permute-start.14 = (bf16[96,2432]{1,0:T(8,128)(2,1)S(1)}, bf16[96,2432]{1,0:T(8,128)(2,1)S(1)}, u32[]{:S(2)}, u32[]{:S(2)}) collective-permute-start(bf16[96,2432]{1,0:T(8,128)(2,1)S(1)} %concatenate.21.refs_0_), channel_id=1, source_target_pairs={{0,16},{16,32},{32,48},{48,0},{1,17},{17,33},{33,49},{49,1},{2,18}... | collective-permute-start | bytes 1400840 | tf_op jit(solution)/shard_map/ppermute | solution.py:27
  35.2 18.4 %collective-permute-start.7 = (bf16[96,4224]{1,0:T(8,128)(2,1)}, bf16[96,4224]{1,0:T(8,128)(2,1)S(1)}, u32[]{:S(2)}, u32[]{:S(2)}) collective-permute-start(bf16[96,4224]{1,0:T(8,128)(2,1)} %stack_kernel.1.refs_0_), channel_id=1, source_target_pairs={{0,66},{2,64},{64,2},{66,0},{1,67},{3,65},{65,3},{67,1},{4,70},{6,... | collective-permute-start | bytes 2433032 | tf_op jit(solution)/shard_map/ppermute | solution.py:26
  38.7 17.9 %collective-permute-start.6 = (bf16[96,4224]{1,0:T(8,128)(2,1)S(1)}, bf16[96,4224]{1,0:T(8,128)(2,1)S(1)}, u32[]{:S(2)}, u32[]{:S(2)}) collective-permute-start(bf16[96,4224]{1,0:T(8,128)(2,1)S(1)} %copy-done.2), channel_id=1, source_target_pairs={{0,64},{2,66},{64,0},{66,2},{1,65},{3,67},{65,1},{67,3},{4,68},{6,... | collective-permute-start | bytes 2433032 | tf_op jit(solution)/shard_map/ppermute | solution.py:26
  45.6 11.9 %collective-permute-start.17 = (bf16[96,2432]{1,0:T(8,128)(2,1)S(1)}, bf16[96,2432]{1,0:T(8,128)(2,1)S(1)}, u32[]{:S(2)}, u32[]{:S(2)}) collective-permute-start(bf16[96,2432]{1,0:T(8,128)(2,1)S(1)} %concatenate.21.refs_0_), channel_id=1, source_target_pairs={{0,1},{1,0},{2,3},{3,2},{4,5},{5,4},{6,7},{7,6},{8,9},{9,8},{10,11... | collective-permute-start | bytes 1400840 | tf_op jit(solution)/shard_map/ppermute | solution.py:21
  45.6 11.9 %collective-permute-start.20 = (bf16[96,2432]{1,0:T(8,128)(2,1)S(1)}, bf16[96,2432]{1,0:T(8,128)(2,1)S(1)}, u32[]{:S(2)}, u32[]{:S(2)}) collective-permute-start(bf16[96,2432]{1,0:T(8,128)(2,1)S(1)} %collective-permute-done.16.refs_3_), channel_id=1, source_target_pairs={{0,1},{1,0},{2,3},{3,2},{4,5},{5,4},{6,7},{7,6},{8,9},{9,8},{10,11... | collective-permute-start | bytes 1400840 | tf_op jit(solution)/shard_map/ppermute | solution.py:21
  56.6 25.6 %collective-permute-start.21 = (bf16[96,4224]{1,0:T(8,128)(2,1)S(1)}, bf16[96,4224]{1,0:T(8,128)(2,1)S(1)}, u32[]{:S(2)}, u32[]{:S(2)}) collective-permute-start(bf16[96,4224]{1,0:T(8,128)(2,1)S(1)} %copy-done.2), channel_id=1, source_target_pairs={{0,2},{2,0},{64,66},{66,64},{1,3},{3,1},{65,67},{67,65},{4,6},{6,4... | collective-permute-start | bytes 2433032 | tf_op jit(solution)/shard_map/ppermute | solution.py:26
  63.7 18.4 %collective-permute-start.22 = (bf16[64,1664]{1,0:T(8,128)(2,1)S(1)}, bf16[64,1664]{1,0:T(8,128)(2,1)S(1)}, u32[]{:S(2)}, u32[]{:S(2)}) collective-permute-start(bf16[64,1664]{1,0:T(8,128)(2,1)S(1)} %get-tuple-element.115), channel_id=1, source_target_pairs={{0,1},{1,2},{2,3},{3,4},{4,5},{5,6},{6,7},{7,8},{8,9},{9,10},{10,1... | collective-permute-start | bytes 638984 | tf_op jit(solution)/shard_map/ppermute | solution.py:563
  66.8 15.4 %collective-permute-start.24 = (bf16[96,4224]{1,0:T(8,128)(2,1)S(1)}, bf16[96,4224]{1,0:T(8,128)(2,1)S(1)}, u32[]{:S(2)}, u32[]{:S(2)}) collective-permute-start(bf16[96,4224]{1,0:T(8,128)(2,1)S(1)} %copy-done.2), channel_id=1, source_target_pairs={{0,1},{1,0},{2,3},{3,2},{4,5},{5,4},{6,7},{7,6},{8,9},{9,8},{10,11... | collective-permute-start | bytes 2433032 | tf_op jit(solution)/shard_map/ppermute | solution.py:21
  69.8 12.4 %collective-permute-start.26 = (bf16[96,4224]{1,0:T(8,128)(2,1)S(1)}, bf16[96,4224]{1,0:T(8,128)(2,1)S(1)}, u32[]{:S(2)}, u32[]{:S(2)}) collective-permute-start(bf16[96,4224]{1,0:T(8,128)(2,1)S(1)} %collective-permute-done.6.refs_2_), channel_id=1, source_target_pairs={{0,1},{1,0},{2,3},{3,2},{4,5},{5,4},{6,7},{7,6},{8,9},{9,8},{10,11... | collective-permute-start | bytes 2433032 | tf_op jit(solution)/shard_map/ppermute | solution.py:21
  69.9 14.1 %collective-permute-start.27 = (bf16[96,4224]{1,0:T(8,128)(2,1)S(1)}, bf16[96,4224]{1,0:T(8,128)(2,1)S(1)}, u32[]{:S(2)}, u32[]{:S(2)}) collective-permute-start(bf16[96,4224]{1,0:T(8,128)(2,1)S(1)} %collective-permute-done.7.refs_3_), channel_id=1, source_target_pairs={{0,1},{1,0},{2,3},{3,2},{4,5},{5,4},{6,7},{7,6},{8,9},{9,8},{10,11... | collective-permute-start | bytes 2433032 | tf_op jit(solution)/shard_map/ppermute | solution.py:21
  108.2 22.6 %collective-permute-start.28 = (bf16[384,4224]{1,0:T(8,128)(2,1)}, bf16[384,4224]{1,0:T(8,128)(2,1)S(1)}, u32[]{:S(2)}, u32[]{:S(2)}) collective-permute-start(bf16[384,4224]{1,0:T(8,128)(2,1)} %get-tuple-element.79), channel_id=1, source_target_pairs={{0,1},{1,0},{2,3},{3,2},{4,5},{5,4},{6,7},{7,6},{8,9},{9,8},{10,11... | collective-permute-start | bytes 9732104 | tf_op jit(solution)/shard_map/ppermute | solution.py:21
  127.4 8.8 %collective-permute-start.29 = (bf16[64,1536]{1,0:T(8,128)(2,1)S(1)}, bf16[64,1536]{1,0:T(8,128)(2,1)S(1)}, u32[]{:S(2)}, u32[]{:S(2)}) collective-permute-start(bf16[64,1536]{1,0:T(8,128)(2,1)S(1)} %get-tuple-element.83), channel_id=1, source_target_pairs={{0,1},{1,2},{2,3},{3,4},{4,5},{5,6},{6,7},{7,8},{8,9},{9,10},{10,1... | collective-permute-start | bytes 589832 | tf_op jit(solution)/shard_map/ppermute | solution.py:614
  136.2 18.7 %collective-permute-start.31 = (bf16[96,4224]{1,0:T(8,128)(2,1)S(1)}, bf16[96,4224]{1,0:T(8,128)(2,1)S(1)}, u32[]{:S(2)}, u32[]{:S(2)}) collective-permute-start(bf16[96,4224]{1,0:T(8,128)(2,1)S(1)} %get-tuple-element.86), channel_id=1, source_target_pairs={{0,64},{2,66},{64,0},{66,2},{1,65},{3,67},{65,1},{67,3},{4,68},{6,... | collective-permute-start | bytes 2433032 | tf_op jit(solution)/shard_map/ppermute | solution.py:26
  136.6 23.9 %collective-permute-start.32 = (bf16[96,4224]{1,0:T(8,128)(2,1)S(1)}, bf16[96,4224]{1,0:T(8,128)(2,1)S(1)}, u32[]{:S(2)}, u32[]{:S(2)}) collective-permute-start(bf16[96,4224]{1,0:T(8,128)(2,1)S(1)} %get-tuple-element.87), channel_id=1, source_target_pairs={{0,66},{2,64},{64,2},{66,0},{1,67},{3,65},{65,3},{67,1},{4,70},{6,... | collective-permute-start | bytes 2433032 | tf_op jit(solution)/shard_map/ppermute | solution.py:26
  150.4 10.1 %collective-permute-start.33 = (bf16[96,2432]{1,0:T(8,128)(2,1)S(1)}, bf16[96,2432]{1,0:T(8,128)(2,1)S(1)}, u32[]{:S(2)}, u32[]{:S(2)}) collective-permute-start(bf16[96,2432]{1,0:T(8,128)(2,1)S(1)} %get-tuple-element.96), channel_id=1, source_target_pairs={{0,1},{1,0},{2,3},{3,2},{4,5},{5,4},{6,7},{7,6},{8,9},{9,8},{10,11... | collective-permute-start | bytes 1400840 | tf_op jit(solution)/shard_map/ppermute | solution.py:21
  150.5 10.0 %collective-permute-start.34 = (bf16[96,2432]{1,0:T(8,128)(2,1)S(1)}, bf16[96,2432]{1,0:T(8,128)(2,1)S(1)}, u32[]{:S(2)}, u32[]{:S(2)}) collective-permute-start(bf16[96,2432]{1,0:T(8,128)(2,1)S(1)} %get-tuple-element.97), channel_id=1, source_target_pairs={{0,1},{1,0},{2,3},{3,2},{4,5},{5,4},{6,7},{7,6},{8,9},{9,8},{10,11... | collective-permute-start | bytes 1400840 | tf_op jit(solution)/shard_map/ppermute | solution.py:21
  151.0 9.5 %collective-permute-start.35 = (bf16[96,2432]{1,0:T(8,128)(2,1)S(1)}, bf16[96,2432]{1,0:T(8,128)(2,1)S(1)}, u32[]{:S(2)}, u32[]{:S(2)}) collective-permute-start(bf16[96,2432]{1,0:T(8,128)(2,1)S(1)} %get-tuple-element.98), channel_id=1, source_target_pairs={{0,1},{1,0},{2,3},{3,2},{4,5},{5,4},{6,7},{7,6},{8,9},{9,8},{10,11... | collective-permute-start | bytes 1400840 | tf_op jit(solution)/shard_map/ppermute | solution.py:21
  162.4 13.7 %collective-permute-start.37 = (bf16[96,2432]{1,0:T(8,128)(2,1)S(1)}, bf16[96,2432]{1,0:T(8,128)(2,1)S(1)}, u32[]{:S(2)}, u32[]{:S(2)}) collective-permute-start(bf16[96,2432]{1,0:T(8,128)(2,1)S(1)} %get-tuple-element.101), channel_id=1, source_target_pairs={{0,48},{16,0},{32,16},{48,32},{1,49},{17,1},{33,17},{49,33},{2,50}... | collective-permute-start | bytes 1400840 | tf_op jit(solution)/shard_map/ppermute | solution.py:27
  164.4 15.2 %collective-permute-start.38 = (bf16[96,2432]{1,0:T(8,128)(2,1)S(1)}, bf16[96,2432]{1,0:T(8,128)(2,1)S(1)}, u32[]{:S(2)}, u32[]{:S(2)}) collective-permute-start(bf16[96,2432]{1,0:T(8,128)(2,1)S(1)} %get-tuple-element.102), channel_id=1, source_target_pairs={{0,32},{16,48},{32,0},{48,16},{1,33},{17,49},{33,1},{49,17},{2,34}... | collective-permute-start | bytes 1400840 | tf_op jit(solution)/shard_map/ppermute | solution.py:27
  165.4 22.1 %collective-permute-start.39 = (bf16[96,2432]{1,0:T(8,128)(2,1)S(1)}, bf16[96,2432]{1,0:T(8,128)(2,1)S(1)}, u32[]{:S(2)}, u32[]{:S(2)}) collective-permute-start(bf16[96,2432]{1,0:T(8,128)(2,1)S(1)} %get-tuple-element.103), channel_id=1, source_target_pairs={{0,16},{16,32},{32,48},{48,0},{1,17},{17,33},{33,49},{49,1},{2,18}... | collective-permute-start | bytes 1400840 | tf_op jit(solution)/shard_map/ppermute | solution.py:27
  166.5 26.8 %collective-permute-start.43 = (bf16[96,4224]{1,0:T(8,128)(2,1)S(1)}, bf16[96,4224]{1,0:T(8,128)(2,1)S(1)}, u32[]{:S(2)}, u32[]{:S(2)}) collective-permute-start(bf16[96,4224]{1,0:T(8,128)(2,1)S(1)} %get-tuple-element.105), channel_id=1, source_target_pairs={{0,2},{2,0},{64,66},{66,64},{1,3},{3,1},{65,67},{67,65},{4,6},{6,4... | collective-permute-start | bytes 2433032 | tf_op jit(solution)/shard_map/ppermute | solution.py:26
  187.8 8.8 %collective-permute-start.40 = (bf16[24,2432]{1,0:T(8,128)(2,1)S(1)}, bf16[24,2432]{1,0:T(8,128)(2,1)S(1)}, u32[]{:S(2)}, u32[]{:S(2)}) collective-permute-start(bf16[24,2432]{1,0:T(8,128)(2,1)S(1)} %get-tuple-element.119), channel_id=1, source_target_pairs={{0,2},{2,0},{64,66},{66,64},{1,3},{3,1},{65,67},{67,65},{4,6},{6,4... | collective-permute-start | bytes 350216 | tf_op jit(solution)/shard_map/ppermute | solution.py:26
  193.7 8.8 %collective-permute-start.44 = (bf16[24,4224]{1,0:T(8,128)(2,1)S(1)}, bf16[24,4224]{1,0:T(8,128)(2,1)S(1)}, u32[]{:S(2)}, u32[]{:S(2)}) collective-permute-start(bf16[24,4224]{1,0:T(8,128)(2,1)S(1)} %get-tuple-element.116), channel_id=1, source_target_pairs={{0,12},{4,0},{8,4},{12,8},{1,13},{5,1},{9,5},{13,9},{2,14},{6,2},{... | collective-permute-start | bytes 608264 | tf_op jit(solution)/shard_map/ppermute | solution.py:27
  196.6 11.4 %collective-permute-start.45 = (bf16[24,4224]{1,0:T(8,128)(2,1)S(1)}, bf16[24,4224]{1,0:T(8,128)(2,1)S(1)}, u32[]{:S(2)}, u32[]{:S(2)}) collective-permute-start(bf16[24,4224]{1,0:T(8,128)(2,1)S(1)} %get-tuple-element.118), channel_id=1, source_target_pairs={{0,8},{4,12},{8,0},{12,4},{1,9},{5,13},{9,1},{13,5},{2,10},{6,14},... | collective-permute-start | bytes 608264 | tf_op jit(solution)/shard_map/ppermute | solution.py:27
  (36 other events, 225.3 us)
